TPU v7x, 128 devices: a whole 4x4x4 slice. The times are simulated.
128 devices in a mesh: row: 8 (over z, core), col: 16 (over y, x).
Axes of the slice: x: 4, y: 4, z: 4, core: 2. Of those that a mesh axis runs over, the one named last changes fastest.
Arguments:
- density: float32 [6144, 6144], P('row', 'col'), as said below
- keep_mask: int32 [48, 48], replicated, may hold values from 0 to 1, as said below
- owner_map: int32 [48], replicated, may hold values from 0 to 7, as said below
Outputs:
- owned_density: float32 [8192, 6144], P('row', 'col')
Inputs may be any that keep to these rules, and one draw needn't show every extreme that they name: density is symmetric. `keep_mask`: symmetric, with ones on the diagonal. `owner_map`: each owner has between 4 and 8 block rows, and 8 is reached; of the 6 block rows k * 6 to k * 6 + 5 at most 2 have one owner, and 2 is reached.
All inputs are finite; a program needn't handle non-finite values.
Results may differ from a plain program's by a relative error of at most 0.0051.
Values may be sent and summed in bfloat16 or wider, within the bound.
A program may use at most 64 MiB of HBM per device.

v0:
```python
import jax
import jax.numpy as jnp
from jax import lax
from jax.sharding import PartitionSpec as P

BS = 128


def fold_product(panel_half, segment):
    return jnp.dot(segment, panel_half, preferred_element_type=jnp.float32)


def body(density, keep_mask, owner_map):
    tile_rows, tile_cols = density.shape
    block_size = BS
    row_count = lax.axis_size("row")
    blocks_down = tile_rows // block_size
    blocks_across = tile_cols // block_size
    row_index = lax.axis_index("row")
    col_index = lax.axis_index("col")
    tile_keep = lax.dynamic_slice(
        keep_mask,
        (row_index * blocks_down, col_index * blocks_across),
        (blocks_down, blocks_across),
    ).astype(jnp.float32)

    def apply_keep(matrix):
        shaped = matrix.reshape(blocks_down, block_size, blocks_across, block_size)
        return (shaped * tile_keep[:, None, :, None]).reshape(tile_rows, tile_cols)

    global_rows = row_index * tile_rows + jnp.arange(tile_rows)
    global_cols = col_index * tile_cols + jnp.arange(tile_cols)
    on_diagonal = global_rows[:, None] == global_cols[None, :]
    electrons = jnp.float32(tile_rows * row_count // 2)
    current = apply_keep(density)
    current_half = current.astype(jnp.bfloat16)
    panel_current = lax.all_gather(current_half, "row", axis=0, tiled=True)
    square = apply_keep(
        fold_product(panel_current, lax.all_gather(current_half, "col", axis=1, tiled=True))
    )
    square_half = square.astype(jnp.bfloat16)
    panel_square = lax.all_gather(square_half, "row", axis=0, tiled=True)
    segment = lax.all_gather(square_half, "col", axis=1, tiled=True)
    cubic_term = fold_product(panel_current, segment)
    quartic = fold_product(panel_square, segment)
    difference = current - square
    local_spread = jnp.sum(difference * difference)
    local_cubic = jnp.sum(jnp.where(on_diagonal, cubic_term, 0.0))
    local_quartic = jnp.sum(jnp.where(on_diagonal, quartic, 0.0))
    total_cubic, total_quartic, spread = lax.psum(
        (local_cubic, local_quartic, local_spread), ("row", "col")
    )
    factor = (electrons - (4.0 * total_cubic - 3.0 * total_quartic)) / (spread + 1e-06)
    current = apply_keep(
        4.0 * cubic_term - 3.0 * quartic + factor * (square - 2.0 * cubic_term + quartic)
    )
    total_blocks = blocks_down * row_count
    capacity = blocks_down + 2
    positions = jnp.arange(total_blocks)
    same_owner = owner_map[:, None] == owner_map[None, :]
    earlier = positions[None, :] < positions[:, None]
    ranking = jnp.sum(same_owner & earlier, axis=1)
    slot_ids = jnp.arange(capacity)
    wanted = (owner_map[None, :] == row_index) & (ranking[None, :] == slot_ids[:, None])
    present = jnp.any(wanted, axis=1)
    source_block = jnp.sum(jnp.where(wanted, positions[None, :], 0), axis=1)
    gathered = lax.all_gather(current, "row", axis=0, tiled=True)
    stacked_rows = gathered.reshape(total_blocks, block_size, tile_cols)
    picked = jnp.take(stacked_rows, source_block, axis=0)
    owned_rows = jnp.where(present[:, None, None], picked, 0.0)
    return owned_rows.reshape(capacity * block_size, tile_cols)


def solution(mesh):
    in_specs = (P("row", "col"), P(), P())
    out_specs = P("row", "col")
    return jax.shard_map(body, mesh=mesh, in_specs=in_specs, out_specs=out_specs, check_vma=False)
```

profile of v0, /device:TPU:1, one launch (start us, length us, event | category | flops | bytes accessed | tf_op | source)
XLA Modules:
  0.0 407.6 jit_solution(10772722390221094166)
XLA Ops:
  6.5 0.8 dynamic-slice_convert_fusion
  7.4 0.2 mul.72
  7.6 0.3 copy.14
  7.9 0.4 copy.9
  8.2 0.9 copy-done
  9.1 1.3 fusion.7
  10.5 0.7 all-gather.6.cloned.1.call-update
  11.3 37.5 %all-gather.8.cloned.1.call-done = bf16[6144,384]{1,0:T(8,128)(2,1)} async-done(((bf16[768,384]{1,0:T(8,128)(2,1)}), bf16[6144,384]{1,0:T(8,128)(2,1)}) %all-gather.8.cloned.1.call-update) | async-done | bytes 4718608 | tf_op jit(solution)/shard_map/all_gather | solution.py:37
  48.8 84.2 %all-gather.6.cloned.1.call-done = bf16[768,6144]{1,0:T(8,128)(2,1)} async-done(((bf16[768,384]{1,0:T(8,128)(2,1)}), bf16[768,6144]{1,0:T(8,128)(2,1)}) %all-gather.6.cloned.1.call-update) | async-done | bytes 9437200 | tf_op jit(solution)/shard_map/all_gather | solution.py:39
  133.0 10.3 %multiply_reduce_fusion = (f32[]{:T(128)}, bf16[768,384]{1,0:T(8,128)(2,1)}, f32[768,384]{1,0:T(8,128)S(1)}) fusion(f32[768,384]{1,0:T(8,128)S(1)} %copy-done.1, f32[768,384]{1,0:T(8,128)S(1)} %copy.9, bf16[768,6144]{1,0:T(8,128)(2,1)} %all-gather.6.cloned.1.call-done, bf16[6144,384]{1,0:T(8,128)(2,1)} %all-gather.8.cloned.1.call-done), kind=kOutput, calls=%fused_computation.10 | convolution fusion | flops 3625353216 | bytes 18284548 | tf_op jit(solution)/shard_map/dot_general | solution.py:10
  143.4 0.5 all-gather.12.cloned.1.call-update
  144.1 82.5 %all-gather.10.cloned.1.call-done = bf16[768,6144]{1,0:T(8,128)(2,1)} async-done(((bf16[768,384]{1,0:T(8,128)(2,1)}), bf16[768,6144]{1,0:T(8,128)(2,1)}) %all-gather.10.cloned.1.call-update) | async-done | bytes 9437200 | tf_op jit(solution)/shard_map/all_gather | solution.py:43
  226.5 9.0 %fusion.8 = f32[768,384]{1,0:T(8,128)S(1)} fusion(bf16[768,6144]{1,0:T(8,128)(2,1)} %all-gather.10.cloned.1.call-done, bf16[6144,384]{1,0:T(8,128)(2,1)} %all-gather.8.cloned.1.call-done), kind=kOutput, calls=%fused_computation.30 | convolution fusion | flops 3623878656 | bytes 15335424 | tf_op jit(solution)/shard_map/dot_general | solution.py:10
  235.5 27.8 %all-gather.12.cloned.1.call-done = bf16[6144,384]{1,0:T(8,128)(2,1)} async-done(((bf16[768,384]{1,0:T(8,128)(2,1)}), bf16[6144,384]{1,0:T(8,128)(2,1)}) %all-gather.12.cloned.1.call-update) | async-done | bytes 4718608 | tf_op jit(solution)/shard_map/all_gather | solution.py:42
  263.3 10.5 %fusion.2 = (f32[]{:T(128)}, f32[]{:T(128)}, f32[768,384]{1,0:T(8,128)}) fusion(s32[384]{0:T(512)S(1)} %iota_add_fusion.1, s32[768]{0:T(1024)S(1)} %iota_add_fusion, f32[768,384]{1,0:T(8,128)S(1)} %fusion.8, bf16[768,6144]{1,0:T(8,128)(2,1)} %all-gather.10.cloned.1.call-done, bf16[6144,384]{1,0:T(8,128)(2,1)} %all-gather.12.cloned.1.call-done), kind=kOutput, calls=%fused_computation.7 | convolution fusion | flops 3625353216 | bytes 16519688 | tf_op jit(solution)/shard_map/dot_general | solution.py:10
  273.8 64.6 %all-reduce = (f32[]{:T(128)}, f32[]{:T(128)}, f32[]{:T(128)}) all-reduce(f32[]{:T(128)} %get-tuple-element.6, f32[]{:T(128)} %get-tuple-element.5, f32[]{:T(128)} %get-tuple-element.12), channel_id=1, replica_groups=mesh['row'=8,'col'=16] {'row','col'}, use_global_device_ids=true, to_apply=%region_4.5 | all-reduce | flops 3 | bytes 24 | tf_op jit(solution)/shard_map/psum | solution.py:50
  340.3 2.6 add_multiply_fusion
  343.0 0.6 copy-done.2
  343.6 0.2 convert_reduce_fusion
  343.8 0.1 select_reduce_fusion
  343.9 0.1 fusion.5
  344.1 51.1 %all-gather.14.cloned.1.call-done = f32[6144,384]{1,0:T(8,128)} async-done(((f32[768,384]{1,0:T(8,128)}), f32[6144,384]{1,0:T(8,128)}) %all-gather.14.cloned.1.call-update) | async-done | bytes 9437200 | tf_op jit(solution)/shard_map/all_gather | solution.py:67
  395.3 4.3 %gather_fusion = f32[8,128,384]{2,1,0:T(8,128)S(1)} fusion(f32[48,128,384]{2,1,0:T(8,128)} %bitcast.28, s32[1024]{0:T(1024)S(1)} %pad_clamp_fusion), kind=kCustom, calls=%fused_computation | custom fusion | bytes 3145760 | tf_op jit(solution)/shard_map/jit(_take)/gather | solution.py:69
  399.6 1.5 fusion
  (20 shorter events, 0.4 us)
Async XLA Ops:
  6.5 42.3 %all-gather.8.cloned.1.call-start = ((), (), s32[]{:S(2)}) async-start(), calls=%async_computation.1 | async-start | bytes 5308416 | tf_op jit(solution)/shard_map/all_gather | solution.py:37
  7.8 1.3 copy-start
  10.5 122.6 %copy-start.1 = (f32[768,384]{1,0:T(8,128)S(1)}, f32[768,384]{1,0:T(8,128)}, u32[]{:S(2)}) copy-start(f32[768,384]{1,0:T(8,128)} %get-tuple-element.11) | copy-start | bytes 3538948
  10.5 122.5 %all-gather.6.cloned.1.call-start = ((), (), s32[]{:S(2)}) async-start(), calls=%async_computation | async-start | bytes 10027008 | tf_op jit(solution)/shard_map/all_gather | solution.py:39
  11.2 215.3 %all-gather.10.cloned.1.call-start = ((), (), s32[]{:S(2)}) async-start(), calls=%async_computation.2 | async-start | bytes 10027008 | tf_op jit(solution)/shard_map/all_gather | solution.py:43
  143.4 119.9 %all-gather.12.cloned.1.call-start = ((), (), s32[]{:S(2)}) async-start(), calls=%async_computation.3 | async-start | bytes 5308416 | tf_op jit(solution)/shard_map/all_gather | solution.py:42
  144.0 251.3 %all-gather.14.cloned.1.call-start = ((), (), s32[]{:S(2)}) async-start(), calls=%async_computation.4 | async-start | bytes 10616832 | tf_op jit(solution)/shard_map/all_gather | solution.py:67
  343.0 0.7 copy-start.2
Sparse Core Ops, SparseCore 0:
  10.6 38.1 all-gather.7
  50.9 82.0 all-gather.5
  143.5 82.9 all-gather.9
  228.1 35.2 all-gather.11
  343.1 52.1 all-gather.13
where the time goes:
time: 408 us
  waiting for transfers between devices  284 us (70%)
  blocking collectives  64.6 us (16%)
  matrix products  29.8 us (7%)
  between operations  15.1 us (4%)
  local copies, waits for them, and re-layouts  6.81 us (2%)
  other arithmetic  6.68 us (2%)
    all_gather x1, waiting for transfers between devices, body(): lax.all_gather(current_half, 'col', axis=1, tiled=True)  84.2 us
    all_gather x1, waiting for transfers between devices, body(): segment = lax.all_gather(square_half, 'col', axis=1, tiled=True)  82.5 us
    psum x1, blocking collectives, body(): lax.psum((local_cubic, local_quartic, local_spread), ('row', 'col'))  64.6 us
    all_gather x1, waiting for transfers between devices, body(): gathered = lax.all_gather(current, 'row', axis=0, tiled=True)  51.1 us
    all_gather x1, waiting for transfers between devices, body(): panel_current = lax.all_gather(current_half, 'row', axis=0, tiled=True)  37.5 us
    dot_general x3, matrix products, fold_product(): return jnp.dot(segment, panel_half, preferred_element_type=jnp.float32)  29.8 us
    all_gather x1, waiting for transfers between devices, body(): panel_square = lax.all_gather(square_half, 'row', axis=0, tiled=True)  27.8 us
  transfers between devices with their start and end apart: 5, of which 5 were waited for; matrix products, arithmetic and copies ran while one was open for 2% of the time, Pallas kernels for 0%

commit v1 on v0

v1 whole, which is shorter than its diff:
```python
import jax
import jax.numpy as jnp
from jax import lax
from jax.experimental import pallas as pl
from jax.experimental.pallas import tpu as pltpu
from jax.sharding import PartitionSpec as P

MESH = pl.DeviceIdType.MESH
F32 = jnp.float32
BF16 = jnp.bfloat16


def kernel(
    dens, keep, owner, out,
    row_c, row_s, col_c, col_s, square, cubic, quartic, moved, sums, sums_in,
    send_sem, row_sem, col_sem, sib_sem, end_sem, end_sib_sem, sum_sem,
):
    rows, cols = dens.shape
    half = rows // 2
    r = lax.axis_index("row")
    c = lax.axis_index("col")
    z, p = r // 2, r % 2
    y, x = c // 4, c % 4
    sign = 1 - 2 * p
    bs = cols // 3
    per = rows // bs

    def at(dz=0, dp=0, dy=0, dx=0):
        return (
            lax.rem(z + dz + 4, 4) * 2 + lax.rem(p + dp, 2),
            lax.rem(y + dy + 4, 4) * 4 + lax.rem(x + dx + 4, 4),
        )

    peers = {}
    for k in (1, 2, 3):
        peers["x", k], peers["y", k], peers["z", k] = at(dx=k), at(dy=k), at(dz=k)
    peers["p", 1] = at(dp=1)
    fwd = {"x": at(dx=sign), "y": at(dy=sign), "z": at(dz=sign)}
    bwd = {"x": at(dx=-sign), "y": at(dy=-sign), "z": at(dz=-sign)}

    barrier = pltpu.get_barrier_semaphore()
    for device in peers.values():
        pl.semaphore_signal(barrier, inc=1, device_id=device, device_id_type=MESH)

    def block(i, j):
        return (slice(i * bs, (i + 1) * bs), slice(j * bs, (j + 1) * bs))

    def kept(i, j):
        return keep[r * per + i, c * 3 + j].astype(F32)

    for i in range(per):
        for j in range(3):
            value = (dens[block(i, j)] * kept(i, j)).astype(BF16)
            h, i2 = divmod(i, per // 2)
            row_c[(h, 0) + block(i2, j)] = value
            col_c[(2 * r + h,) + block(i2, j)] = value

    pl.semaphore_wait(barrier, len(peers))

    started = []

    def send(src, dst, recv, device):
        copy = pltpu.make_async_remote_copy(
            src_ref=src, dst_ref=dst, send_sem=send_sem.at[len(started)],
            recv_sem=recv, device_id=device, device_id_type=MESH,
        )
        copy.start()
        started.append(copy)

    def arrived(dst, recv):
        pltpu.make_async_remote_copy(
            src_ref=dst, dst_ref=dst, send_sem=send_sem.at[0],
            recv_sem=recv, device_id=peers["p", 1], device_id_type=MESH,
        ).wait_recv()

    def slot(h, first, second):
        return 4 * second + first if h == 0 else 4 * first + second

    def gather(stage, row, col, product, on_round):
        routes = (("x", "y"), ("y", "x"))

        def pass_on(h, first, second, which, direction):
            step = 1 if direction is fwd else 3
            there = ((first + step) % 4, second) if which == 0 else (first, (second + step) % 4)
            goal = slot(h, *there)
            send(
                row.at[h, slot(h, first, second)], row.at[h, goal],
                row_sem.at[stage, h, goal], direction[routes[h][which]],
            )

        def have(h, first, second):
            if second == 0:
                if first == 0:
                    pass_on(h, 0, 0, 0, fwd)
                    pass_on(h, 0, 0, 0, bwd)
                    return
                if first == 1:
                    pass_on(h, 1, 0, 0, fwd)
                second_stage(h, first)
            elif second == 1:
                pass_on(h, first, 1, 1, fwd)

        def second_stage(h, first):
            pass_on(h, first, 0, 1, fwd)
            pass_on(h, first, 0, 1, bwd)

        def columns(core, away, lane_sign):
            source = lax.rem(z - lane_sign * away + 8, 4) * 2 + core
            return col.at[pl.ds(2 * source, 2)]

        def have_col(away):
            piece = columns(p, away, sign)
            for step, direction in ((1, fwd), (3, bwd)):
                if away == 0 or (away == 1 and step == 1):
                    send(piece, piece, col_sem.at[stage, (away + step) % 4], direction["z"])
            send(piece, piece, sib_sem.at[stage, away], peers["p", 1])

        waiting = []

        def multiply(count):
            for _ in range(min(count, len(waiting))):
                h, first, second = waiting.pop(0)
                place = slot(h, first, second)
                behind_y, behind_x = divmod(place, 4)
                k = lax.rem(y - sign * behind_y + 8, 4) * 4 + lax.rem(x - sign * behind_x + 8, 4)
                product(h, row.at[h, place], k)

        for h in range(2):
            have(h, 0, 0)
        have_col(0)
        for h in range(2):
            second_stage(h, 0)
        waiting += [(0, 0, 0), (1, 0, 0)]
        order = (
            ((1, 0), (3, 0)),
            ((0, 1), (0, 3)),
            ((2, 0),),
            ((1, 1), (3, 1), (1, 3), (3, 3)),
            ((0, 2), (2, 1), (2, 3)),
            ((1, 2), (3, 2)),
            ((2, 2),),
        )
        for number, pieces in enumerate(order):
            for first, second in pieces:
                for h in range(2):
                    place = slot(h, first, second)
                    arrived(row.at[h, place], row_sem.at[stage, h, place])
                    have(h, first, second)
                    waiting.append((h, first, second))
                    if number > 2:
                        multiply(2)
                if number in (0, 2):
                    arrived(columns(p, first, sign), col_sem.at[stage, first])
                    have_col(first)
            if number == 2:
                for away in range(4):
                    arrived(columns(1 - p, away, -sign), sib_sem.at[stage, away])
            on_round(number)
        multiply(len(waiting))

    def add(total, h, a, b):
        here = pl.ds(h * half, half)
        total[here, :] += jnp.dot(a[...], b, preferred_element_type=F32)

    def first_product(h, piece, k):
        add(square, h, piece, col_c[k])

    def second_product(h, piece, k):
        add(cubic, h, piece, col_c[k])
        add(quartic, h, piece, col_s[k])

    square[...] = jnp.zeros_like(square)
    cubic[...] = jnp.zeros_like(cubic)
    quartic[...] = jnp.zeros_like(quartic)

    gather(0, row_c, col_c, first_product, lambda number: None)

    fold = lambda v: jnp.sum(v.reshape(bs // 8, 8, bs), axis=0)
    totals = [jnp.zeros((8, bs), F32)] * 3
    for i in range(per):
        for j in range(3):
            mask = kept(i, j)
            value = square[block(i, j)] * mask
            square[block(i, j)] = value
            rounded = value.astype(BF16)
            h, i2 = divmod(i, per // 2)
            row_s[(h, 0) + block(i2, j)] = rounded
            col_s[(2 * r + h,) + block(i2, j)] = rounded
            difference = dens[block(i, j)] * mask - value
            wide = rounded.astype(F32)
            one = row_c[(h, 0) + block(i2, j)].astype(F32)
            terms = (wide * one, wide * wide, difference * difference)
            totals = [t + fold(v) for t, v in zip(totals, terms, strict=True)]
    for n in range(3):
        sums[0, n] = totals[n]

    def reduce_start(step, axis, count):
        for k in range(1, count):
            send(sums.at[step], sums_in.at[step, k - 1], sum_sem.at[step, k - 1], peers[axis, k])

    def reduce_end(step, count):
        total = sums[step]
        for k in range(1, count):
            arrived(sums_in.at[step, k - 1], sum_sem.at[step, k - 1])
            total += sums_in[step, k - 1]
        sums[step + 1] = total

    axes = (("z", 4), ("p", 2), ("x", 4), ("y", 4))

    def on_round(number):
        if 0 < number < 5:
            reduce_end(number - 1, axes[number - 1][1])
        if number < 4:
            reduce_start(number, *axes[number])

    gather(1, row_s, col_s, second_product, on_round)

    trace_cubic, trace_quartic, spread = (
        jnp.sum(sums[4, n], keepdims=True) for n in range(3)
    )
    electrons = F32(rows * 8 // 2)
    factor = (electrons - (4.0 * trace_cubic - 3.0 * trace_quartic)) / (spread + 1e-06)
    for i in range(per):
        for j in range(3):
            three, four = cubic[block(i, j)], quartic[block(i, j)]
            value = 4.0 * three - 3.0 * four + factor * (square[block(i, j)] - 2.0 * three + four)
            moved[r * per + i, :, j * bs:(j + 1) * bs] = (value * kept(i, j)).astype(BF16)

    def moved_rows(core, away, lane_sign):
        source = lax.rem(z - lane_sign * away + 8, 4) * 2 + core
        return moved.at[pl.ds(source * per, per)]

    for away in (0, 1, 3, 2):
        piece = moved_rows(p, away, sign)
        if away:
            arrived(piece, end_sem.at[away])
        for step, direction in ((1, fwd), (3, bwd)):
            if away == 0 or (away == 1 and step == 1):
                send(piece, piece, end_sem.at[(away + step) % 4], direction["z"])
        send(piece, piece, end_sib_sem.at[away], peers["p", 1])

    slots = out.shape[0] // bs

    def place(i, state):
        count, sources = state
        mine = jnp.where(owner[i] == r, 1, 0)
        sources = tuple(
            jnp.where((mine == 1) & (count == s), i, v) for s, v in enumerate(sources)
        )
        return count + mine, sources

    count, sources = lax.fori_loop(
        0, 8 * per, place, (jnp.int32(0), (jnp.int32(0),) * slots)
    )
    for away in range(4):
        arrived(moved_rows(1 - p, away, -sign), end_sib_sem.at[away])
    for s in range(slots):
        rows_of_slot = moved[sources[s]].astype(F32)
        out[s * bs:(s + 1) * bs, :] = jnp.where(s < count, rows_of_slot, 0.0)
    for copy in started:
        copy.wait_send()


def step(density, keep_mask, owner_map):
    rows, cols = density.shape
    half, bs = rows // 2, cols // 3
    per = rows // bs
    dma = pltpu.SemaphoreType.DMA
    return pl.pallas_call(
        kernel,
        out_shape=jax.ShapeDtypeStruct(((per + 2) * bs, cols), F32),
        in_specs=[
            pl.BlockSpec(memory_space=pltpu.VMEM),
            pl.BlockSpec(memory_space=pltpu.SMEM),
            pl.BlockSpec(memory_space=pltpu.SMEM),
        ],
        out_specs=pl.BlockSpec(memory_space=pltpu.VMEM),
        scratch_shapes=[
            pltpu.VMEM((2, 16, half, cols), BF16),
            pltpu.VMEM((2, 16, half, cols), BF16),
            pltpu.VMEM((16, half, cols), BF16),
            pltpu.VMEM((16, half, cols), BF16),
            pltpu.VMEM((rows, cols), F32),
            pltpu.VMEM((rows, cols), F32),
            pltpu.VMEM((rows, cols), F32),
            pltpu.VMEM((8 * per, bs, cols), BF16),
            pltpu.VMEM((5, 3, 8, bs), F32),
            pltpu.VMEM((4, 3, 3, 8, bs), F32),
            dma((96,)),
            dma((2, 2, 16)),
            dma((2, 4)),
            dma((2, 4)),
            dma((4,)),
            dma((4,)),
            dma((4, 3)),
        ],
        compiler_params=pltpu.CompilerParams(
            collective_id=0, has_side_effects=True, vmem_limit_bytes=56 << 20
        ),
    )(density, keep_mask, owner_map)


def solution(mesh):
    return jax.shard_map(
        step,
        mesh=mesh,
        in_specs=(P("row", "col"), P(), P()),
        out_specs=P("row", "col"),
        check_vma=False,
    )
```

time: 408 us -> 142 us (0.35)
  waiting for transfers between devices: 284 us -> 0 us
  Pallas kernels: 0 us -> 139 us
  blocking collectives: 64.6 us -> 0 us
  matrix products: 29.8 us -> 0 us
  between operations: 15.1 us -> 0.01 us
  other arithmetic: 6.68 us -> 0 us
  local copies, waits for them, and re-layouts: 6.81 us -> 2.65 us
    all_gather x5 -> x0, waiting for transfers between devices: 283 us -> none  [the longest x1 84.2 us: body(): lax.all_gather(current_half, 'col', axis=1, tiled=True)]
    pallas_call x0 -> x1, Pallas kernels: none -> 139 us  [step(): pl.pallas_call(kernel, out_shape=jax.ShapeDtypeStruct(((per + 2) * bs, co...]
    psum x1 -> x0, blocking collectives: 64.6 us -> none  [body(): lax.psum((local_cubic, local_quartic, local_spread), ('row', 'col'))]
    dot_general x3 -> x0, matrix products: 29.8 us -> none  [fold_product(): return jnp.dot(segment, panel_half, preferred_element_type=jnp.float32)]
    gather x1 -> x0, local copies, waits for them, and re-layouts: 4.33 us -> none  [body(): picked = jnp.take(stacked_rows, source_block, axis=0)]
  transfers between devices with their start and end apart: 5 -> 0, of which waited for: 5 -> 0; matrix products, arithmetic and copies ran while one was open for 2% -> 0% of each run, Pallas kernels for 0% -> 0%
where the time goes in v1:
time: 142 us
  Pallas kernels  139 us (98%)
  local copies, waits for them, and re-layouts  2.65 us (2%)
    pallas_call x1, Pallas kernels, step(): pl.pallas_call(kernel, out_shape=jax.ShapeDtypeStruct(((per + 2) * bs, co...  139 us

profile of v1, /device:TPU:1, one launch (start us, length us, event | category | flops | bytes accessed | tf_op | source)
XLA Modules:
  0.0 141.6 jit_solution(13400952325035658764)
XLA Ops:
  0.0 139.0 %shard_map.37 = f32[1024,384]{1,0:T(8,128)} custom-call(f32[768,384]{1,0:T(8,128)} %dens.1, s32[48,48]{1,0:T(8,128)} %keep.1, s32[48]{0:T(128)} %owner.1), custom_call_target="tpu_custom_call" | custom-call | tf_op jit(solution)/shard_map/pallas_call | solution.py:269
  139.0 2.7 %copy.5 = f32[1024,384]{1,0:T(8,128)} copy(f32[1024,384]{1,0:T(8,128)} %shard_map.37) | data formatting | bytes 3145728

commit v2 on v1

v2 whole, which is shorter than its diff:
```python
import jax
import jax.numpy as jnp
from jax import lax
from jax.experimental import pallas as pl
from jax.experimental.pallas import tpu as pltpu
from jax.sharding import PartitionSpec as P

MESH = pl.DeviceIdType.MESH
F32 = jnp.float32
BF16 = jnp.bfloat16


def kernel(
    dens, keep, owner, out,
    row_c, row_s, col_c, col_s, square, cubic, quartic, moved, sums, sums_in,
    send_sem, row_sem, col_sem, sib_sem, end_sem, end_sib_sem, sum_sem,
):
    rows, cols = dens.shape
    group = rows // 2
    half = group // 2
    r = lax.axis_index("row")
    c = lax.axis_index("col")
    z, p = r // 2, r % 2
    y, x = c // 4, c % 4
    sign = 1 - 2 * p
    bs = cols // 3
    per = rows // bs
    per_group = per // 2

    def at(dz=0, dp=0, dy=0, dx=0):
        return (
            lax.rem(z + dz + 4, 4) * 2 + lax.rem(p + dp, 2),
            lax.rem(y + dy + 4, 4) * 4 + lax.rem(x + dx + 4, 4),
        )

    sibling = at(dp=1)
    fwd = {"x": at(dx=sign), "y": at(dy=sign), "z": at(dz=sign)}
    bwd = {"x": at(dx=-sign), "y": at(dy=-sign), "z": at(dz=-sign)}
    reduce_peers = (
        [at(dz=k // 2, dp=k % 2) for k in range(1, 8)],
        [at(dx=k) for k in range(1, 4)],
        [at(dy=k) for k in range(1, 4)],
    )

    barrier = pltpu.get_barrier_semaphore()
    for devices in reduce_peers:
        for device in devices:
            pl.semaphore_signal(barrier, inc=1, device_id=device, device_id_type=MESH)

    def block(i, j):
        return (slice(i * bs, (i + 1) * bs), slice(j * bs, (j + 1) * bs))

    def kept(i, j):
        return keep[r * per + i, c * 3 + j].astype(F32)

    for i in range(per):
        for j in range(3):
            value = (dens[block(i, j)] * kept(i, j)).astype(BF16)
            g, inner = divmod(i, per_group)
            row_c[(g, 0) + block(inner, j)] = value
            col_c[(2 * r + g,) + block(inner, j)] = value

    pl.semaphore_wait(barrier, sum(len(devices) for devices in reduce_peers))

    started = []

    def send(src, dst, recv, device):
        copy = pltpu.make_async_remote_copy(
            src_ref=src, dst_ref=dst, send_sem=send_sem.at[len(started)],
            recv_sem=recv, device_id=device, device_id_type=MESH,
        )
        copy.start()
        started.append(copy)

    def arrived(dst, recv):
        pltpu.make_async_remote_copy(
            src_ref=dst, dst_ref=dst, send_sem=send_sem.at[0],
            recv_sem=recv, device_id=sibling, device_id_type=MESH,
        ).wait_recv()

    pending = []

    def work(count):
        for _ in range(min(count, len(pending))):
            pending.pop(0)()

    order = (
        ((1, 0), (3, 0)),
        ((0, 1), (0, 3)),
        ((2, 0),),
        ((1, 1), (3, 1), (1, 3), (3, 3)),
        ((0, 2), (2, 1), (2, 3)),
        ((1, 2), (3, 2)),
        ((2, 2),),
    )
    routes = (("x", "y"), ("y", "x"))

    def slot(h, first, second):
        return 4 * second + first if h == 0 else 4 * first + second

    class Rows:
        def __init__(self, stage, g, row, ready):
            self.stage, self.g, self.row, self.ready, self.halves = stage, g, row, ready, {}

        def piece(self, h, place):
            return self.row.at[self.g, place, pl.ds(h * half, half)]

        def pass_on(self, h, first, second, which, direction):
            n = 1 if direction is fwd else 3
            there = ((first + n) % 4, second) if which == 0 else (first, (second + n) % 4)
            goal = slot(h, *there)
            send(
                self.piece(h, slot(h, first, second)), self.piece(h, goal),
                row_sem.at[self.stage, self.g, h, goal], direction[routes[h][which]],
            )

        def turn(self, h, first):
            self.pass_on(h, first, 0, 1, fwd)
            self.pass_on(h, first, 0, 1, bwd)

        def start(self):
            for h in range(2):
                self.pass_on(h, 0, 0, 0, fwd)
                self.pass_on(h, 0, 0, 0, bwd)
            for h in range(2):
                self.turn(h, 0)
            self.ready(self.g, 0)

        def round(self, number, effort=1):
            for first, second in order[number]:
                for h in range(2):
                    place = slot(h, first, second)
                    arrived(self.piece(h, place), row_sem.at[self.stage, self.g, h, place])
                    if second == 0:
                        if first == 1:
                            self.pass_on(h, 1, 0, 0, fwd)
                        self.turn(h, first)
                    elif second == 1:
                        self.pass_on(h, first, 1, 1, fwd)
                    self.halves[place] = self.halves.get(place, 0) + 1
                    if self.halves[place] == 2:
                        self.ready(self.g, place)
                    work(effort)

    class Ring:
        def __init__(self, piece, own, shared):
            self.piece, self.own, self.shared = piece, own, shared

        def at(self, core, away, lane_sign):
            return self.piece(lax.rem(z - lane_sign * away + 8, 4) * 2 + core)

        def have(self, away):
            here = self.at(p, away, sign)
            for n, direction in ((1, fwd), (3, bwd)):
                if away == 0 or (away == 1 and n == 1):
                    send(here, here, self.own.at[(away + n) % 4], direction["z"])
            send(here, here, self.shared.at[away], sibling)

        def take(self, *aways):
            for away in aways:
                arrived(self.at(p, away, sign), self.own.at[away])
                self.have(away)

        def finish(self):
            for away in range(4):
                arrived(self.at(1 - p, away, -sign), self.shared.at[away])

    def column_ring(stage, g, col):
        return Ring(lambda source: col.at[2 * source + g], col_sem.at[stage, g], sib_sem.at[stage, g])

    def move_ring(g):
        return Ring(
            lambda source: moved.at[pl.ds(source * per + g * per_group, per_group)],
            end_sem.at[g], end_sib_sem.at[g],
        )

    def column_of(place):
        behind_y, behind_x = divmod(place, 4)
        return lax.rem(y - sign * behind_y + 8, 4) * 4 + lax.rem(x - sign * behind_x + 8, 4)

    fresh = set()

    def add(name, total, g, place, row, col):
        here = pl.ds(g * group, group)
        term = jnp.dot(row[g, place], col[column_of(place)], preferred_element_type=F32)
        if (name, g) in fresh:
            total[here, :] += term
        else:
            fresh.add((name, g))
            total[here, :] = term

    waiting_c, waiting_s = [], []

    def ready_c(g, place):
        waiting_c.append(lambda: add("square", square, g, place, row_c, col_c))
        if columns_c:
            pending.append(waiting_c.pop())

    def ready_s(g, place):
        pending.append(lambda: add("cubic", cubic, g, place, row_s, col_c))
        waiting_s.append(lambda: add("quartic", quartic, g, place, row_s, col_s))
        if columns_s:
            pending.append(waiting_s.pop())

    columns_c, columns_s = [], []

    def fold(v):
        return jnp.sum(v.reshape(bs // 8, 8, bs), axis=0)

    totals = [jnp.zeros((8, bs), F32)] * 3

    def make_square(g):
        work(len(pending))
        for i in range(g * per_group, (g + 1) * per_group):
            for j in range(3):
                value = square[block(i, j)] * kept(i, j)
                square[block(i, j)] = value
                rounded = value.astype(BF16)
                inner = i - g * per_group
                row_s[(g, 0) + block(inner, j)] = rounded
                col_s[(2 * r + g,) + block(inner, j)] = rounded

    def add_sums(g):
        for i in range(g * per_group, (g + 1) * per_group):
            for j in range(3):
                inner = i - g * per_group
                value = square[block(i, j)]
                difference = dens[block(i, j)] * kept(i, j) - value
                wide = row_s[(g, 0) + block(inner, j)].astype(F32)
                one = row_c[(g, 0) + block(inner, j)].astype(F32)
                terms = (wide * one, wide * wide, difference * difference)
                for n, v in enumerate(terms):
                    totals[n] = totals[n] + fold(v)

    def reduce_start(n):
        for k, device in enumerate(reduce_peers[n]):
            send(sums.at[n], sums_in.at[n, k], sum_sem.at[n, k], device)

    def reduce_end(n):
        total = sums[n]
        for k in range(len(reduce_peers[n])):
            arrived(sums_in.at[n, k], sum_sem.at[n, k])
            total += sums_in[n, k]
        sums[n + 1] = total

    def make_result(g):
        work(len(pending))
        trace_cubic, trace_quartic, spread = (
            jnp.sum(sums[3, n], keepdims=True) for n in range(3)
        )
        electrons = F32(rows * 8 // 2)
        factor = (electrons - (4.0 * trace_cubic - 3.0 * trace_quartic)) / (spread + 1e-06)
        for i in range(g * per_group, (g + 1) * per_group):
            for j in range(3):
                three, four = cubic[block(i, j)], quartic[block(i, j)]
                value = 4.0 * three - 3.0 * four + factor * (square[block(i, j)] - 2.0 * three + four)
                moved[r * per + i, :, j * bs:(j + 1) * bs] = (value * kept(i, j)).astype(BF16)

    c0, c1 = (Rows(0, g, row_c, ready_c) for g in range(2))
    s0, s1 = (Rows(1, g, row_s, ready_s) for g in range(2))
    zc0, zc1 = (column_ring(0, g, col_c) for g in range(2))
    zs0, zs1 = (column_ring(1, g, col_s) for g in range(2))
    m0, m1 = (move_ring(g) for g in range(2))

    c0.start()
    zc0.have(0)
    zc1.have(0)
    c0.round(0)
    zc0.take(1, 3)
    c0.round(1)
    zc1.take(1, 3)
    c0.round(2)
    zc0.take(2)
    c1.start()
    c0.round(3)
    zc1.take(2)
    zc0.finish()
    zc1.finish()
    columns_c.append(True)
    pending += waiting_c
    waiting_c.clear()
    c0.round(4, 2)
    c1.round(0, 2)
    c0.round(5, 2)
    c1.round(1, 2)
    c0.round(6, 2)
    make_square(0)
    zs0.have(0)
    c1.round(2)
    s0.start()
    c1.round(3)
    add_sums(0)
    c1.round(4)
    zs0.take(1, 3)
    s0.round(0)
    c1.round(5)
    c1.round(6)
    make_square(1)
    zs1.have(0)
    add_sums(1)
    for n in range(3):
        sums[0, n] = totals[n]
    reduce_start(0)
    zs0.take(2)
    s0.round(1)
    reduce_end(0)
    reduce_start(1)
    s0.round(2)
    zs1.take(1, 3)
    s1.start()
    reduce_end(1)
    reduce_start(2)
    s0.round(3)
    zs1.take(2)
    zs0.finish()
    zs1.finish()
    columns_s.append(True)
    pending += waiting_s
    waiting_s.clear()
    s0.round(4, 3)
    reduce_end(2)
    s1.round(0, 3)
    s0.round(5, 3)
    s1.round(1, 3)
    s0.round(6, 3)
    make_result(0)
    m0.have(0)
    s1.round(2, 2)
    s1.round(3, 2)
    m0.take(1, 3)
    s1.round(4, 2)
    s1.round(5, 2)
    m0.take(2)
    s1.round(6, 2)
    make_result(1)
    m1.have(0)

    slots = out.shape[0] // bs

    def place(i, state):
        count, sources = state
        mine = jnp.where(owner[i] == r, 1, 0)
        sources = tuple(
            jnp.where((mine == 1) & (count == s), i, v) for s, v in enumerate(sources)
        )
        return count + mine, sources

    count, sources = lax.fori_loop(
        0, 8 * per, place, (jnp.int32(0), (jnp.int32(0),) * slots)
    )
    m1.take(1, 3, 2)
    m0.finish()
    m1.finish()
    for s in range(slots):
        found = moved[sources[s]]
        out[s * bs:(s + 1) * bs, :] = jnp.where(s < count, found, jnp.zeros_like(found))
    for copy in started:
        copy.wait_send()


def step(density, keep_mask, owner_map):
    rows, cols = density.shape
    group, bs = rows // 2, cols // 3
    per = rows // bs
    dma = pltpu.SemaphoreType.DMA
    return pl.pallas_call(
        kernel,
        out_shape=jax.ShapeDtypeStruct(((per + 2) * bs, cols), BF16),
        in_specs=[
            pl.BlockSpec(memory_space=pltpu.VMEM),
            pl.BlockSpec(memory_space=pltpu.SMEM),
            pl.BlockSpec(memory_space=pltpu.SMEM),
        ],
        out_specs=pl.BlockSpec(memory_space=pltpu.VMEM),
        scratch_shapes=[
            pltpu.VMEM((2, 16, group, cols), BF16),
            pltpu.VMEM((2, 16, group, cols), BF16),
            pltpu.VMEM((16, group, cols), BF16),
            pltpu.VMEM((16, group, cols), BF16),
            pltpu.VMEM((rows, cols), F32),
            pltpu.VMEM((rows, cols), F32),
            pltpu.VMEM((rows, cols), F32),
            pltpu.VMEM((8 * per, bs, cols), BF16),
            pltpu.VMEM((4, 3, 8, bs), F32),
            pltpu.VMEM((3, 7, 3, 8, bs), F32),
            dma((180,)),
            dma((2, 2, 2, 16)),
            dma((2, 2, 4)),
            dma((2, 2, 4)),
            dma((2, 4)),
            dma((2, 4)),
            dma((3, 7)),
        ],
        compiler_params=pltpu.CompilerParams(
            collective_id=0, has_side_effects=True, vmem_limit_bytes=56 << 20
        ),
    )(density, keep_mask, owner_map).astype(F32)


def solution(mesh):
    return jax.shard_map(
        step,
        mesh=mesh,
        in_specs=(P("row", "col"), P(), P()),
        out_specs=P("row", "col"),
        check_vma=False,
    )
```

time: 142 us -> 135 us (0.951)
  Pallas kernels: 139 us -> 132 us
  local copies, waits for them, and re-layouts: 2.65 us -> 0 us
  other arithmetic: 0 us -> 2.38 us
    pallas_call x1, Pallas kernels: 139 us -> 132 us  [step(): pl.pallas_call(kernel, out_shape=jax.ShapeDtypeStruct(((per + 2) * bs, co...]
    unnamed x1 -> x0, local copies, waits for them, and re-layouts: 2.65 us -> none
    convert_element_type x0 -> x1, other arithmetic: none -> 2.38 us  [step(): return pl.pallas_call(kernel, out_shape=jax.ShapeDtypeStruct(((per + 2) *...]
where the time goes in v2:
time: 135 us
  Pallas kernels  132 us (98%)
  other arithmetic  2.38 us (2%)
    pallas_call x1, Pallas kernels, step(): pl.pallas_call(kernel, out_shape=jax.ShapeDtypeStruct(((per + 2) * bs, co...  132 us

profile of v2, /device:TPU:1, one launch (start us, length us, event | category | flops | bytes accessed | tf_op | source)
XLA Modules:
  0.0 134.8 jit_solution(5541526661080680022)
XLA Ops:
  0.0 132.4 %shard_map.37 = bf16[1024,384]{1,0:T(8,128)(2,1)} custom-call(f32[768,384]{1,0:T(8,128)} %dens.1, s32[48,48]{1,0:T(8,128)} %keep.1, s32[48]{0:T(128)} %owner.1), custom_call_target="tpu_custom_call" | custom-call | tf_op jit(solution)/shard_map/pallas_call | solution.py:366
  132.4 2.4 %convert_element_type.3 = f32[1024,384]{1,0:T(8,128)} convert(bf16[1024,384]{1,0:T(8,128)(2,1)} %shard_map.37) | non-fusion elementwise | flops 393216 | bytes 2359296 | tf_op jit(solution)/shard_map/convert_element_type | solution.py:397

commit v3 on v2

--- a/solution.py
+++ b/solution.py
@@ -10,7 +10,7 @@
 BF16 = jnp.bfloat16
 
 
-def kernel(
+def dense_kernel(
     dens, keep, owner, out,
     row_c, row_s, col_c, col_s, square, cubic, quartic, moved, sums, sums_in,
     send_sem, row_sem, col_sem, sib_sem, end_sem, end_sib_sem, sum_sem,
@@ -78,12 +78,6 @@
             recv_sem=recv, device_id=sibling, device_id_type=MESH,
         ).wait_recv()
 
-    pending = []
-
-    def work(count):
-        for _ in range(min(count, len(pending))):
-            pending.pop(0)()
-
     order = (
         ((1, 0), (3, 0)),
         ((0, 1), (0, 3)),
@@ -99,8 +93,8 @@
         return 4 * second + first if h == 0 else 4 * first + second
 
     class Rows:
-        def __init__(self, stage, g, row, ready):
-            self.stage, self.g, self.row, self.ready, self.halves = stage, g, row, ready, {}
+        def __init__(self, stage, g, row):
+            self.stage, self.g, self.row = stage, g, row
 
         def piece(self, h, place):
             return self.row.at[self.g, place, pl.ds(h * half, half)]
@@ -124,9 +118,8 @@
                 self.pass_on(h, 0, 0, 0, bwd)
             for h in range(2):
                 self.turn(h, 0)
-            self.ready(self.g, 0)
-
-        def round(self, number, effort=1):
+
+        def round(self, number):
             for first, second in order[number]:
                 for h in range(2):
                     place = slot(h, first, second)
@@ -137,10 +130,6 @@
                         self.turn(h, first)
                     elif second == 1:
                         self.pass_on(h, first, 1, 1, fwd)
-                    self.halves[place] = self.halves.get(place, 0) + 1
-                    if self.halves[place] == 2:
-                        self.ready(self.g, place)
-                    work(effort)
 
     class Ring:
         def __init__(self, piece, own, shared):
@@ -174,35 +163,19 @@
             end_sem.at[g], end_sib_sem.at[g],
         )
 
-    def column_of(place):
-        behind_y, behind_x = divmod(place, 4)
-        return lax.rem(y - sign * behind_y + 8, 4) * 4 + lax.rem(x - sign * behind_x + 8, 4)
-
-    fresh = set()
-
-    def add(name, total, g, place, row, col):
+    def multiply(g, row, *pairs):
         here = pl.ds(g * group, group)
-        term = jnp.dot(row[g, place], col[column_of(place)], preferred_element_type=F32)
-        if (name, g) in fresh:
-            total[here, :] += term
-        else:
-            fresh.add((name, g))
-            total[here, :] = term
-
-    waiting_c, waiting_s = [], []
-
-    def ready_c(g, place):
-        waiting_c.append(lambda: add("square", square, g, place, row_c, col_c))
-        if columns_c:
-            pending.append(waiting_c.pop())
-
-    def ready_s(g, place):
-        pending.append(lambda: add("cubic", cubic, g, place, row_s, col_c))
-        waiting_s.append(lambda: add("quartic", quartic, g, place, row_s, col_s))
-        if columns_s:
-            pending.append(waiting_s.pop())
-
-    columns_c, columns_s = [], []
+        for total, _ in pairs:
+            total[here, :] = jnp.zeros((group, cols), F32)
+
+        def one(place, carry):
+            behind_y, behind_x = place // 4, place % 4
+            k = lax.rem(y - sign * behind_y + 8, 4) * 4 + lax.rem(x - sign * behind_x + 8, 4)
+            for total, col in pairs:
+                total[here, :] += jnp.dot(row[g, place], col[k], preferred_element_type=F32)
+            return carry
+
+        lax.fori_loop(0, 16, one, 0)
 
     def fold(v):
         return jnp.sum(v.reshape(bs // 8, 8, bs), axis=0)
@@ -210,7 +183,7 @@
     totals = [jnp.zeros((8, bs), F32)] * 3
 
     def make_square(g):
-        work(len(pending))
+        multiply(g, row_c, (square, col_c))
         for i in range(g * per_group, (g + 1) * per_group):
             for j in range(3):
                 value = square[block(i, j)] * kept(i, j)
@@ -244,7 +217,7 @@
         sums[n + 1] = total
 
     def make_result(g):
-        work(len(pending))
+        multiply(g, row_s, (cubic, col_c), (quartic, col_s))
         trace_cubic, trace_quartic, spread = (
             jnp.sum(sums[3, n], keepdims=True) for n in range(3)
         )
@@ -256,8 +229,8 @@
                 value = 4.0 * three - 3.0 * four + factor * (square[block(i, j)] - 2.0 * three + four)
                 moved[r * per + i, :, j * bs:(j + 1) * bs] = (value * kept(i, j)).astype(BF16)
 
-    c0, c1 = (Rows(0, g, row_c, ready_c) for g in range(2))
-    s0, s1 = (Rows(1, g, row_s, ready_s) for g in range(2))
+    c0, c1 = (Rows(0, g, row_c) for g in range(2))
+    s0, s1 = (Rows(1, g, row_s) for g in range(2))
     zc0, zc1 = (column_ring(0, g, col_c) for g in range(2))
     zs0, zs1 = (column_ring(1, g, col_s) for g in range(2))
     m0, m1 = (move_ring(g) for g in range(2))
@@ -276,14 +249,11 @@
     zc1.take(2)
     zc0.finish()
     zc1.finish()
-    columns_c.append(True)
-    pending += waiting_c
-    waiting_c.clear()
-    c0.round(4, 2)
-    c1.round(0, 2)
-    c0.round(5, 2)
-    c1.round(1, 2)
-    c0.round(6, 2)
+    c0.round(4)
+    c1.round(0)
+    c0.round(5)
+    c1.round(1)
+    c0.round(6)
     make_square(0)
     zs0.have(0)
     c1.round(2)
@@ -314,24 +284,21 @@
     zs1.take(2)
     zs0.finish()
     zs1.finish()
-    columns_s.append(True)
-    pending += waiting_s
-    waiting_s.clear()
-    s0.round(4, 3)
+    s0.round(4)
     reduce_end(2)
-    s1.round(0, 3)
-    s0.round(5, 3)
-    s1.round(1, 3)
-    s0.round(6, 3)
+    s1.round(0)
+    s0.round(5)
+    s1.round(1)
+    s0.round(6)
     make_result(0)
     m0.have(0)
-    s1.round(2, 2)
-    s1.round(3, 2)
+    s1.round(2)
+    s1.round(3)
     m0.take(1, 3)
-    s1.round(4, 2)
-    s1.round(5, 2)
+    s1.round(4)
+    s1.round(5)
     m0.take(2)
-    s1.round(6, 2)
+    s1.round(6)
     make_result(1)
     m1.have(0)
 
@@ -358,13 +325,13 @@
         copy.wait_send()
 
 
-def step(density, keep_mask, owner_map):
+def dense_step(density, keep_mask, owner_map):
     rows, cols = density.shape
     group, bs = rows // 2, cols // 3
     per = rows // bs
     dma = pltpu.SemaphoreType.DMA
     return pl.pallas_call(
-        kernel,
+        dense_kernel,
         out_shape=jax.ShapeDtypeStruct(((per + 2) * bs, cols), BF16),
         in_specs=[
             pl.BlockSpec(memory_space=pltpu.VMEM),
@@ -392,9 +359,403 @@
             dma((3, 7)),
         ],
         compiler_params=pltpu.CompilerParams(
+            collective_id=1, has_side_effects=True, vmem_limit_bytes=56 << 20
+        ),
+    )(density, keep_mask, owner_map)
+
+
+LIST = 12
+
+
+def packed_kernel(
+    dens, keep, owner, out,
+    blocks, col_c, col_s, left, square, cubic, quartic, moved, sums, sums_in, spots, spots_here,
+    send_sem, row_sem, col_sem, sib_sem, end_sem, end_sib_sem, sum_sem, *lists,
+):
+    rows, cols = dens.shape
+    bs = cols // 3
+    per = rows // bs
+    tile = per * 3
+    list_c, list_s = lists[:16], lists[16:]
+    half = LIST // 2
+    r = lax.axis_index("row")
+    c = lax.axis_index("col")
+    z, p = r // 2, r % 2
+    y, x = c // 4, c % 4
+    sign = 1 - 2 * p
+
+    def at(dz=0, dp=0, dy=0, dx=0):
+        return (
+            lax.rem(z + dz + 4, 4) * 2 + lax.rem(p + dp, 2),
+            lax.rem(y + dy + 4, 4) * 4 + lax.rem(x + dx + 4, 4),
+        )
+
+    sibling = at(dp=1)
+    fwd = {"x": at(dx=sign), "y": at(dy=sign), "z": at(dz=sign)}
+    bwd = {"x": at(dx=-sign), "y": at(dy=-sign), "z": at(dz=-sign)}
+    reduce_peers = (
+        [at(dz=k // 2, dp=k % 2) for k in range(1, 8)],
+        [at(dy=k // 4, dx=k % 4) for k in range(1, 16)],
+    )
+
+    barrier = pltpu.get_barrier_semaphore()
+    for devices in reduce_peers:
+        for device in devices:
+            pl.semaphore_signal(barrier, inc=1, device_id=device, device_id_type=MESH)
+
+    def block(i, j):
+        return (slice(i * bs, (i + 1) * bs), slice(j * bs, (j + 1) * bs))
+
+    def kept(i, j):
+        return keep[r * per + i, c * 3 + j].astype(F32)
+
+    def col_block(i, j):
+        return (2 * r + i // (per // 2),) + block(i % (per // 2), j)
+
+    for i in range(per):
+        for j in range(3):
+            value = (dens[block(i, j)] * kept(i, j)).astype(BF16)
+            blocks[i * 3 + j] = value
+            col_c[col_block(i, j)] = value
+
+    def find(b, state):
+        count, sources = state
+        one = keep[r * per + b // 3, c * 3 + b % 3]
+        sources = tuple(
+            jnp.where((one == 1) & (count == s), b, v) for s, v in enumerate(sources)
+        )
+        return count + one, sources
+
+    _, listed = lax.fori_loop(0, tile, find, (jnp.int32(0), (jnp.int32(0),) * LIST))
+
+    def pack(target):
+        for s in range(LIST):
+            target[s] = blocks[listed[s]]
+
+    pack(list_c[0])
+    pl.semaphore_wait(barrier, sum(len(devices) for devices in reduce_peers))
+
+    started = []
+
+    def send(src, dst, recv, device):
+        copy = pltpu.make_async_remote_copy(
+            src_ref=src, dst_ref=dst, send_sem=send_sem.at[len(started)],
+            recv_sem=recv, device_id=device, device_id_type=MESH,
+        )
+        copy.start()
+        started.append(copy)
+
+    def arrived(dst, recv):
+        pltpu.make_async_remote_copy(
+            src_ref=dst, dst_ref=dst, send_sem=send_sem.at[0],
+            recv_sem=recv, device_id=sibling, device_id_type=MESH,
+        ).wait_recv()
+
+    pending = []
+
+    def work(count):
+        for _ in range(min(count, len(pending))):
+            pending.pop(0)()
+
+    routes = (("x", "y"), ("y", "x"))
+
+    def slot(h, first, second):
+        return 4 * second + first if h == 0 else 4 * first + second
+
+    class Rows:
+        def __init__(self, stage, row, ready):
+            self.stage, self.row, self.ready, self.halves = stage, row, ready, {}
+
+        def piece(self, h, place):
+            return self.row[place].at[pl.ds(h * half, half)]
+
+        def pass_on(self, h, first, second, which, direction):
+            n = 1 if direction is fwd else 3
+            there = ((first + n) % 4, second) if which == 0 else (first, (second + n) % 4)
+            goal = slot(h, *there)
+            send(
+                self.piece(h, slot(h, first, second)), self.piece(h, goal),
+                row_sem.at[self.stage, h, goal], direction[routes[h][which]],
+            )
+
+        def turn(self, h, first):
+            self.pass_on(h, first, 0, 1, fwd)
+            self.pass_on(h, first, 0, 1, bwd)
+
+        def start(self):
+            for h in range(2):
+                self.pass_on(h, 0, 0, 0, fwd)
+                self.pass_on(h, 0, 0, 0, bwd)
+            for h in range(2):
+                self.turn(h, 0)
+            self.ready(0)
+
+        def take(self, *pieces, effort=1):
+            for first, second in pieces:
+                for h in range(2):
+                    place = slot(h, first, second)
+                    arrived(self.piece(h, place), row_sem.at[self.stage, h, place])
+                    if second == 0:
+                        if first == 1:
+                            self.pass_on(h, 1, 0, 0, fwd)
+                        self.turn(h, first)
+                    elif second == 1:
+                        self.pass_on(h, first, 1, 1, fwd)
+                    self.halves[place] = self.halves.get(place, 0) + 1
+                    if self.halves[place] == 2:
+                        self.ready(place)
+                    work(effort)
+
+    class Ring:
+        def __init__(self, piece, own, shared):
+            self.piece, self.own, self.shared = piece, own, shared
+
+        def at(self, core, away, lane_sign):
+            return self.piece(lax.rem(z - lane_sign * away + 8, 4) * 2 + core)
+
+        def have(self, away):
+            here = self.at(p, away, sign)
+            for n, direction in ((1, fwd), (3, bwd)):
+                if away == 0 or (away == 1 and n == 1):
+                    send(here, here, self.own.at[(away + n) % 4], direction["z"])
+            send(here, here, self.shared.at[away], sibling)
+
+        def take(self, *aways):
+            for away in aways:
+                arrived(self.at(p, away, sign), self.own.at[away])
+                self.have(away)
+
+        def finish(self):
+            for away in range(4):
+                arrived(self.at(1 - p, away, -sign), self.shared.at[away])
+
+    def columns(stage, col):
+        return Ring(lambda source: col.at[pl.ds(2 * source, 2)], col_sem.at[stage], sib_sem.at[stage])
+
+    def column_of(place):
+        behind_y, behind_x = divmod(place, 4)
+        return lax.rem(y - sign * behind_y + 8, 4) * 4 + lax.rem(x - sign * behind_x + 8, 4)
+
+    def spread(row, place):
+        source = column_of(place)
+        for i in range(per):
+            for j in range(3):
+                found = row[place][spots[source * tile + i * 3 + j]]
+                there = keep[r * per + i, source * 3 + j] == 1
+                left[block(i, j)] = jnp.where(there, found, jnp.zeros_like(found))
+
+    fresh = set()
+
+    def add(name, total, place, col):
+        term = jnp.dot(left[...], col[column_of(place)], preferred_element_type=F32)
+        if name in fresh:
+            total[...] += term
+        else:
+            fresh.add(name)
+            total[...] = term
+
+    waiting = []
+    columns_ready = []
+
+    def first_product(place):
+        spread(list_c, place)
+        add("square", square, place, col_c)
+
+    def second_product(place):
+        spread(list_s, place)
+        add("cubic", cubic, place, col_c)
+        add("quartic", quartic, place, col_s)
+
+    def ready_for(product):
+        def ready(place):
+            waiting.append(lambda: product(place))
+            if columns_ready:
+                pending.append(waiting.pop())
+        return ready
+
+    def now_columns():
+        columns_ready.append(True)
+        pending.extend(waiting)
+        waiting.clear()
+
+    rows_c = Rows(0, list_c, ready_for(first_product))
+    rows_s = Rows(1, list_s, ready_for(second_product))
+    ring_c, ring_s = columns(0, col_c), columns(1, col_s)
+
+    rows_c.start()
+    ring_c.have(0)
+
+    def number(t, count):
+        count = jnp.where(t % tile == 0, 0, count)
+        spots[t] = jnp.minimum(count, LIST - 1)
+        return count + keep[r * per + t % tile // 3, t // tile * 3 + t % 3]
+
+    lax.fori_loop(0, 16 * tile, number, jnp.int32(0))
+
+    rows_c.take((1, 0), (3, 0))
+    ring_c.take(1, 3)
+    rows_c.take((0, 1), (0, 3))
+    rows_c.take((2, 0))
+    ring_c.take(2)
+    rows_c.take((1, 1), (3, 1), (1, 3), (3, 3))
+    ring_c.finish()
+    now_columns()
+    rows_c.take((0, 2), (2, 1), (2, 3), effort=2)
+    rows_c.take((1, 2), (3, 2), effort=2)
+    rows_c.take((2, 2), effort=2)
+    work(len(pending))
+    columns_ready.clear()
+
+    for i in range(per):
+        for j in range(3):
+            value = square[block(i, j)] * kept(i, j)
+            square[block(i, j)] = value
+            rounded = value.astype(BF16)
+            col_s[col_block(i, j)] = rounded
+            blocks[i * 3 + j] = rounded
+    pack(list_s[0])
+    rows_s.start()
+    ring_s.have(0)
+
+    def fold(v):
+        return jnp.sum(v.reshape(bs // 8, 8, bs), axis=0)
+
+    totals = [jnp.zeros((8, bs), F32)] * 3
+    for i in range(per):
+        for j in range(3):
+            value = square[block(i, j)]
+            difference = dens[block(i, j)] * kept(i, j) - value
+            wide = blocks[i * 3 + j].astype(F32)
+            one = col_c[col_block(i, j)].astype(F32)
+            terms = (wide * one, wide * wide, difference * difference)
+            totals = [t + fold(v) for t, v in zip(totals, terms, strict=True)]
+    sums[0] = jnp.zeros((8, bs), F32)
+    for n in range(3):
+        sums[0, n:n + 1] = jnp.sum(totals[n], axis=0, keepdims=True)
+
+    def reduce_start(n):
+        for k, device in enumerate(reduce_peers[n]):
+            send(sums.at[n], sums_in.at[n, k], sum_sem.at[n, k], device)
+
+    def reduce_end(n):
+        total = sums[n]
+        for k in range(len(reduce_peers[n])):
+            arrived(sums_in.at[n, k], sum_sem.at[n, k])
+            total += sums_in[n, k]
+        sums[n + 1] = total
+
+    reduce_start(0)
+    rows_s.take((1, 0), (3, 0))
+    ring_s.take(1, 3)
+    rows_s.take((0, 1), (0, 3))
+    rows_s.take((2, 0))
+    ring_s.take(2)
+    rows_s.take((1, 1), (3, 1), (1, 3), (3, 3))
+    reduce_end(0)
+    reduce_start(1)
+    ring_s.finish()
+    now_columns()
+    rows_s.take((0, 2), (2, 1), (2, 3), effort=2)
+    rows_s.take((1, 2), (3, 2), effort=2)
+    rows_s.take((2, 2), effort=2)
+    work(len(pending))
+    reduce_end(1)
+
+    trace_cubic, trace_quartic, spread_sum = (
+        jnp.sum(sums[2, n:n + 1], keepdims=True) for n in range(3)
+    )
+    electrons = F32(rows * 8 // 2)
+    factor = (electrons - (4.0 * trace_cubic - 3.0 * trace_quartic)) / (spread_sum + 1e-06)
+    for i in range(per):
+        for j in range(3):
+            three, four = cubic[block(i, j)], quartic[block(i, j)]
+            value = 4.0 * three - 3.0 * four + factor * (square[block(i, j)] - 2.0 * three + four)
+            blocks[i * 3 + j] = (value * kept(i, j)).astype(BF16)
+    for s in range(LIST):
+        moved[r * LIST + s] = blocks[listed[s]]
+    ring_t = Ring(lambda source: moved.at[pl.ds(source * LIST, LIST)], end_sem, end_sib_sem)
+    ring_t.have(0)
+
+    slots = out.shape[0] // bs
+
+    def number_here(t, count):
+        count = jnp.where(t % tile == 0, 0, count)
+        spots_here[t] = jnp.minimum(count, LIST - 1) + t // tile * LIST
+        return count + keep[t // 3, c * 3 + t % 3]
+
+    lax.fori_loop(0, 8 * tile, number_here, jnp.int32(0))
+
+    def place_rows(i, state):
+        count, sources = state
+        one = jnp.where(owner[i] == r, 1, 0)
+        sources = tuple(
+            jnp.where((one == 1) & (count == s), i, v) for s, v in enumerate(sources)
+        )
+        return count + one, sources
+
+    count, sources = lax.fori_loop(
+        0, 8 * per, place_rows, (jnp.int32(0), (jnp.int32(0),) * slots)
+    )
+    ring_t.take(1, 3, 2)
+    ring_t.finish()
+    for s in range(slots):
+        for j in range(3):
+            found = moved[spots_here[sources[s] * 3 + j]]
+            there = (s < count) & (keep[sources[s], c * 3 + j] == 1)
+            out[block(s, j)] = jnp.where(there, found, jnp.zeros_like(found))
+    for copy in started:
+        copy.wait_send()
+
+
+def packed_step(density, keep_mask, owner_map):
+    rows, cols = density.shape
+    bs = cols // 3
+    per = rows // bs
+    dma = pltpu.SemaphoreType.DMA
+    return pl.pallas_call(
+        packed_kernel,
+        out_shape=jax.ShapeDtypeStruct(((per + 2) * bs, cols), BF16),
+        in_specs=[
+            pl.BlockSpec(memory_space=pltpu.VMEM),
+            pl.BlockSpec(memory_space=pltpu.SMEM),
+            pl.BlockSpec(memory_space=pltpu.SMEM),
+        ],
+        out_specs=pl.BlockSpec(memory_space=pltpu.VMEM),
+        scratch_shapes=[
+            pltpu.VMEM((per * 3, bs, bs), BF16),
+            pltpu.VMEM((16, cols, cols), BF16),
+            pltpu.VMEM((16, cols, cols), BF16),
+            pltpu.VMEM((rows, cols), BF16),
+            pltpu.VMEM((rows, cols), F32),
+            pltpu.VMEM((rows, cols), F32),
+            pltpu.VMEM((rows, cols), F32),
+            pltpu.VMEM((8 * LIST, bs, bs), BF16),
+            pltpu.VMEM((3, 8, bs), F32),
+            pltpu.VMEM((2, 15, 8, bs), F32),
+            pltpu.SMEM((16 * per * 3,), jnp.int32),
+            pltpu.SMEM((8 * per * 3,), jnp.int32),
+            dma((108,)),
+            dma((2, 2, 16)),
+            dma((2, 4)),
+            dma((2, 4)),
+            dma((4,)),
+            dma((4,)),
+            dma((2, 15)),
+        ] + [pltpu.VMEM((LIST, bs, bs), BF16)] * 32,
+        compiler_params=pltpu.CompilerParams(
             collective_id=0, has_side_effects=True, vmem_limit_bytes=56 << 20
         ),
-    )(density, keep_mask, owner_map).astype(F32)
+    )(density, keep_mask, owner_map)
+
+
+def step(density, keep_mask, owner_map):
+    rows = lax.axis_size("row")
+    cols = lax.axis_size("col")
+    blocks = keep_mask.shape[0]
+    kept = keep_mask.reshape(rows, blocks // rows, cols, blocks // cols).sum(axis=(1, 3))
+    return lax.cond(
+        jnp.max(kept) <= LIST, packed_step, dense_step, density, keep_mask, owner_map
+    ).astype(F32)
 
 
 def solution(mesh):

time: 135 us -> 114 us (0.84)
  Pallas kernels: 132 us -> 110 us
    pallas_call x1, Pallas kernels: 132 us -> 110 us  [packed_step(): pl.pallas_call(packed_kernel, out_shape=jax.ShapeDtypeStruct(((per + 2) *...]
where the time goes in v3:
time: 114 us
  Pallas kernels  110 us (96%)
  other arithmetic  2.23 us (2%)
    pallas_call x1, Pallas kernels, packed_step(): pl.pallas_call(packed_kernel, out_shape=jax.ShapeDtypeStruct(((per + 2) *...  110 us

profile of v3, /device:TPU:1, one launch (start us, length us, event | category | flops | bytes accessed | tf_op | source)
XLA Modules:
  0.0 113.7 jit_solution(3336490583358673683)
XLA Ops:
  0.0 0.8 copy.5
  0.8 0.1 reshape.3
  0.9 0.3 reduce_sum.9
  1.3 0.6 reduce_max.9
  2.6 109.8 %conditional.6 = (bf16[1024,384]{1,0:T(8,128)(2,1)S(1)}) conditional(s32[]{:T(128)} %convert_element_type.12, (f32[768,384]{1,0:T(8,128)}, s32[48,48]{1,0:T(8,128)}, s32[48]{0:T(128)}) %tuple.21, (f32[768,384]{1,0:T(8,128)}, s32[48,48]{1,0:T(8,128)}, s32[48]{0:T(128)}) %tuple.21), branch_computations={%region_2.0_spmd, %region_3.0_spmd} | conditional | bytes 8
  2.6 109.5 %branch_1_fun.1 = bf16[1024,384]{1,0:T(8,128)(2,1)S(1)} custom-call(f32[768,384]{1,0:T(8,128)} %get-tuple-element.29.dens, s32[48,48]{1,0:T(8,128)} %get-tuple-element.30.keep, s32[48]{0:T(128)} %get-tuple-element.31.owner), custom_call_target="tpu_custom_call" | custom-call | tf_op jit(solution)/shard_map/cond/branch_1_fun/pallas_call | solution.py:715
  112.4 1.2 %convert_element_type.13 = f32[1024,384]{1,0:T(8,128)} convert(bf16[1024,384]{1,0:T(8,128)(2,1)S(1)} %get-tuple-element.32) | non-fusion elementwise | flops 393216 | bytes 2359296 | tf_op jit(solution)/shard_map/convert_element_type | solution.py:758

commit v4 on v3

--- a/solution.py
+++ b/solution.py
@@ -364,20 +364,26 @@
     )(density, keep_mask, owner_map)
 
 
-LIST = 12
+LIST = 7
+BUNDLE = 18
 
 
 def packed_kernel(
     dens, keep, owner, out,
-    blocks, col_c, col_s, left, square, cubic, quartic, moved, sums, sums_in, spots, spots_here,
+    blocks, col_c, col_s, left, square, cubic, quartic, moved, sums, sums_in, spots, spots_here, counts, offsets,
     send_sem, row_sem, col_sem, sib_sem, end_sem, end_sib_sem, sum_sem, *lists,
 ):
     rows, cols = dens.shape
     bs = cols // 3
     per = rows // bs
     tile = per * 3
-    list_c, list_s = lists[:16], lists[16:]
-    half = LIST // 2
+    part = tile // 2
+
+    def origin(i):
+        return i % (per // 2) * 2 + i // (per // 2)
+
+    list_c, list_s = lists[0:2], lists[2:4]
+    bundle_c, bundle_s = (lists[4:8], lists[8:12]), (lists[12:16], lists[16:20])
     r = lax.axis_index("row")
     c = lax.axis_index("col")
     z, p = r // 2, r % 2
@@ -407,32 +413,35 @@
         return (slice(i * bs, (i + 1) * bs), slice(j * bs, (j + 1) * bs))
 
     def kept(i, j):
-        return keep[r * per + i, c * 3 + j].astype(F32)
+        return keep[r * per + origin(i), c * 3 + j].astype(F32)
 
     def col_block(i, j):
-        return (2 * r + i // (per // 2),) + block(i % (per // 2), j)
+        return (2 * r + origin(i) // (per // 2),) + block(origin(i) % (per // 2), j)
 
     for i in range(per):
         for j in range(3):
-            value = (dens[block(i, j)] * kept(i, j)).astype(BF16)
+            value = (dens[block(origin(i), j)] * kept(i, j)).astype(BF16)
             blocks[i * 3 + j] = value
             col_c[col_block(i, j)] = value
 
-    def find(b, state):
-        count, sources = state
-        one = keep[r * per + b // 3, c * 3 + b % 3]
-        sources = tuple(
-            jnp.where((one == 1) & (count == s), b, v) for s, v in enumerate(sources)
-        )
-        return count + one, sources
-
-    _, listed = lax.fori_loop(0, tile, find, (jnp.int32(0), (jnp.int32(0),) * LIST))
-
-    def pack(target):
-        for s in range(LIST):
-            target[s] = blocks[listed[s]]
-
-    pack(list_c[0])
+    def find(h):
+        count, sources = jnp.int32(0), [jnp.int32(h * part)] * LIST
+        for b in range(h * part, (h + 1) * part):
+            one = keep[r * per + origin(b // 3), c * 3 + b % 3]
+            sources = [
+                jnp.where((one == 1) & (count == s), b, v) for s, v in enumerate(sources)
+            ]
+            count = count + one
+        return sources
+
+    listed = [find(0), find(1)]
+
+    def pack(targets):
+        for h in range(2):
+            for s in range(LIST):
+                targets[h][s] = blocks[listed[h][s]]
+
+    pack(list_c)
     pl.semaphore_wait(barrier, sum(len(devices) for devices in reduce_peers))
 
     started = []
@@ -459,52 +468,51 @@
 
     routes = (("x", "y"), ("y", "x"))
 
-    def slot(h, first, second):
-        return 4 * second + first if h == 0 else 4 * first + second
-
     class Rows:
-        def __init__(self, stage, row, ready):
-            self.stage, self.row, self.ready, self.halves = stage, row, ready, {}
-
-        def piece(self, h, place):
-            return self.row[place].at[pl.ds(h * half, half)]
-
-        def pass_on(self, h, first, second, which, direction):
-            n = 1 if direction is fwd else 3
-            there = ((first + n) % 4, second) if which == 0 else (first, (second + n) % 4)
-            goal = slot(h, *there)
-            send(
-                self.piece(h, slot(h, first, second)), self.piece(h, goal),
-                row_sem.at[self.stage, h, goal], direction[routes[h][which]],
-            )
-
-        def turn(self, h, first):
-            self.pass_on(h, first, 0, 1, fwd)
-            self.pass_on(h, first, 0, 1, bwd)
+        def __init__(self, stage, lists, bundles, ready):
+            self.stage, self.lists, self.bundles, self.ready = stage, lists, bundles, ready
+
+        def piece(self, ring, h, away):
+            if ring == 0:
+                return self.lists[h].at[pl.ds(away * LIST, LIST)]
+            return self.bundles[h][away]
+
+        def have(self, ring, h, away):
+            for n, direction in ((1, fwd), (3, bwd)):
+                if away == 0 or (away == 1 and n == 1):
+                    goal = (away + n) % 4
+                    send(
+                        self.piece(ring, h, away), self.piece(ring, h, goal),
+                        row_sem.at[self.stage, ring, h, goal], direction[routes[h][ring]],
+                    )
 
         def start(self):
             for h in range(2):
-                self.pass_on(h, 0, 0, 0, fwd)
-                self.pass_on(h, 0, 0, 0, bwd)
+                self.have(0, h, 0)
+
+        def take(self, ring, *aways):
+            for away in aways:
+                for h in range(2):
+                    arrived(self.piece(ring, h, away), row_sem.at[self.stage, ring, h, away])
+                    self.have(ring, h, away)
+                    if ring == 1:
+                        self.ready(h, away)
+
+        def bundle(self):
             for h in range(2):
-                self.turn(h, 0)
-            self.ready(0)
-
-        def take(self, *pieces, effort=1):
-            for first, second in pieces:
-                for h in range(2):
-                    place = slot(h, first, second)
-                    arrived(self.piece(h, place), row_sem.at[self.stage, h, place])
-                    if second == 0:
-                        if first == 1:
-                            self.pass_on(h, 1, 0, 0, fwd)
-                        self.turn(h, first)
-                    elif second == 1:
-                        self.pass_on(h, first, 1, 1, fwd)
-                    self.halves[place] = self.halves.get(place, 0) + 1
-                    if self.halves[place] == 2:
-                        self.ready(place)
-                    work(effort)
+                place = x if h == 0 else y
+                starts = [
+                    offsets[h * 16 + (4 * y + t if h == 0 else 4 * t + x)] for t in range(4)
+                ]
+                label = [lax.rem(sign * (place - t) + 8, 4) * LIST for t in range(4)]
+                for s in range(BUNDLE):
+                    shift = label[0]
+                    for t in range(1, 4):
+                        shift = jnp.where(s >= starts[t], label[t] - starts[t], shift)
+                    source = jnp.minimum(jnp.maximum(s + shift, 0), 4 * LIST - 1)
+                    self.bundles[h][0][s] = self.lists[h][source]
+                self.have(1, h, 0)
+                self.ready(h, 0)
 
     class Ring:
         def __init__(self, piece, own, shared):
@@ -536,41 +544,48 @@
         behind_y, behind_x = divmod(place, 4)
         return lax.rem(y - sign * behind_y + 8, 4) * 4 + lax.rem(x - sign * behind_x + 8, 4)
 
-    def spread(row, place):
+    def spread(bundles, h, place):
         source = column_of(place)
-        for i in range(per):
+        start = offsets[h * 16 + source]
+        bundle = bundles[h][place // 4 if h == 0 else place % 4]
+        for i in range(h * per // 2, (h + 1) * per // 2):
             for j in range(3):
-                found = row[place][spots[source * tile + i * 3 + j]]
-                there = keep[r * per + i, source * 3 + j] == 1
+                spot = jnp.minimum(start + spots[source * tile + i * 3 + j], BUNDLE - 1)
+                found = bundle[spot]
+                there = keep[r * per + origin(i), source * 3 + j] == 1
                 left[block(i, j)] = jnp.where(there, found, jnp.zeros_like(found))
 
     fresh = set()
 
-    def add(name, total, place, col):
-        term = jnp.dot(left[...], col[column_of(place)], preferred_element_type=F32)
-        if name in fresh:
-            total[...] += term
+    def add(name, total, h, place, col):
+        here = pl.ds(h * (rows // 2), rows // 2)
+        term = jnp.dot(left[here, :], col[column_of(place)], preferred_element_type=F32)
+        if (name, h) in fresh:
+            total[here, :] += term
         else:
-            fresh.add(name)
-            total[...] = term
+            fresh.add((name, h))
+            total[here, :] = term
 
     waiting = []
     columns_ready = []
 
-    def first_product(place):
-        spread(list_c, place)
-        add("square", square, place, col_c)
-
-    def second_product(place):
-        spread(list_s, place)
-        add("cubic", cubic, place, col_c)
-        add("quartic", quartic, place, col_s)
+    def first_product(h, place):
+        spread(bundle_c, h, place)
+        add("square", square, h, place, col_c)
+
+    def second_product(h, place):
+        spread(bundle_s, h, place)
+        add("cubic", cubic, h, place, col_c)
+        add("quartic", quartic, h, place, col_s)
 
     def ready_for(product):
-        def ready(place):
-            waiting.append(lambda: product(place))
+        def ready(h, away):
+            for other in range(4):
+                place = 4 * away + other if h == 0 else 4 * other + away
+                waiting.append(lambda place=place: product(h, place))
             if columns_ready:
-                pending.append(waiting.pop())
+                pending.extend(waiting)
+                waiting.clear()
         return ready
 
     def now_columns():
@@ -578,31 +593,42 @@
         pending.extend(waiting)
         waiting.clear()
 
-    rows_c = Rows(0, list_c, ready_for(first_product))
-    rows_s = Rows(1, list_s, ready_for(second_product))
+    rows_c = Rows(0, list_c, bundle_c, ready_for(first_product))
+    rows_s = Rows(1, list_s, bundle_s, ready_for(second_product))
     ring_c, ring_s = columns(0, col_c), columns(1, col_s)
 
     rows_c.start()
     ring_c.have(0)
 
-    def number(t, count):
-        count = jnp.where(t % tile == 0, 0, count)
-        spots[t] = jnp.minimum(count, LIST - 1)
-        return count + keep[r * per + t % tile // 3, t // tile * 3 + t % 3]
-
-    lax.fori_loop(0, 16 * tile, number, jnp.int32(0))
-
-    rows_c.take((1, 0), (3, 0))
+    def number(source, carry):
+        for h in range(2):
+            count = jnp.int32(0)
+            for b in range(h * part, (h + 1) * part):
+                spots[source * tile + b] = count
+                count = count + keep[r * per + origin(b // 3), source * 3 + b % 3]
+            counts[2 * source + h] = count
+        return carry
+
+    lax.fori_loop(0, 16, number, 0)
+    for h in range(2):
+        for i in range(4):
+            start = jnp.int32(0)
+            for t in range(4):
+                source = 4 * i + t if h == 0 else 4 * t + i
+                offsets[h * 16 + source] = start
+                start = start + counts[2 * source + h]
+
+    rows_c.take(0, 1, 3, 2)
+    rows_c.bundle()
     ring_c.take(1, 3)
-    rows_c.take((0, 1), (0, 3))
-    rows_c.take((2, 0))
     ring_c.take(2)
-    rows_c.take((1, 1), (3, 1), (1, 3), (3, 3))
+    rows_c.take(1, 1)
     ring_c.finish()
     now_columns()
-    rows_c.take((0, 2), (2, 1), (2, 3), effort=2)
-    rows_c.take((1, 2), (3, 2), effort=2)
-    rows_c.take((2, 2), effort=2)
+    work(12)
+    rows_c.take(1, 3)
+    work(len(pending))
+    rows_c.take(1, 2)
     work(len(pending))
     columns_ready.clear()
 
@@ -613,7 +639,7 @@
             rounded = value.astype(BF16)
             col_s[col_block(i, j)] = rounded
             blocks[i * 3 + j] = rounded
-    pack(list_s[0])
+    pack(list_s)
     rows_s.start()
     ring_s.have(0)
 
@@ -624,7 +650,7 @@
     for i in range(per):
         for j in range(3):
             value = square[block(i, j)]
-            difference = dens[block(i, j)] * kept(i, j) - value
+            difference = dens[block(origin(i), j)] * kept(i, j) - value
             wide = blocks[i * 3 + j].astype(F32)
             one = col_c[col_block(i, j)].astype(F32)
             terms = (wide * one, wide * wide, difference * difference)
@@ -645,19 +671,19 @@
         sums[n + 1] = total
 
     reduce_start(0)
-    rows_s.take((1, 0), (3, 0))
+    rows_s.take(0, 1, 3, 2)
+    rows_s.bundle()
     ring_s.take(1, 3)
-    rows_s.take((0, 1), (0, 3))
-    rows_s.take((2, 0))
     ring_s.take(2)
-    rows_s.take((1, 1), (3, 1), (1, 3), (3, 3))
+    rows_s.take(1, 1)
     reduce_end(0)
     reduce_start(1)
     ring_s.finish()
     now_columns()
-    rows_s.take((0, 2), (2, 1), (2, 3), effort=2)
-    rows_s.take((1, 2), (3, 2), effort=2)
-    rows_s.take((2, 2), effort=2)
+    work(8)
+    rows_s.take(1, 3)
+    work(len(pending))
+    rows_s.take(1, 2)
     work(len(pending))
     reduce_end(1)
 
@@ -671,19 +697,23 @@
             three, four = cubic[block(i, j)], quartic[block(i, j)]
             value = 4.0 * three - 3.0 * four + factor * (square[block(i, j)] - 2.0 * three + four)
             blocks[i * 3 + j] = (value * kept(i, j)).astype(BF16)
-    for s in range(LIST):
-        moved[r * LIST + s] = blocks[listed[s]]
-    ring_t = Ring(lambda source: moved.at[pl.ds(source * LIST, LIST)], end_sem, end_sib_sem)
+    for h in range(2):
+        for s in range(LIST):
+            moved[(2 * r + h) * LIST + s] = blocks[listed[h][s]]
+    ring_t = Ring(lambda source: moved.at[pl.ds(2 * source * LIST, 2 * LIST)], end_sem, end_sib_sem)
     ring_t.have(0)
 
     slots = out.shape[0] // bs
 
-    def number_here(t, count):
-        count = jnp.where(t % tile == 0, 0, count)
-        spots_here[t] = jnp.minimum(count, LIST - 1) + t // tile * LIST
-        return count + keep[t // 3, c * 3 + t % 3]
-
-    lax.fori_loop(0, 8 * tile, number_here, jnp.int32(0))
+    def number_here(source, carry):
+        for h in range(2):
+            count = jnp.int32(0)
+            for b in range(h * part, (h + 1) * part):
+                spots_here[source * tile + b] = jnp.minimum(count, LIST - 1) + (2 * source + h) * LIST
+                count = count + keep[source * per + origin(b // 3), c * 3 + b % 3]
+        return carry
+
+    lax.fori_loop(0, 8, number_here, 0)
 
     def place_rows(i, state):
         count, sources = state
@@ -700,7 +730,9 @@
     ring_t.finish()
     for s in range(slots):
         for j in range(3):
-            found = moved[spots_here[sources[s] * 3 + j]]
+            inner = sources[s] % per
+            at_place = sources[s] - inner + inner % 2 * (per // 2) + inner // 2
+            found = moved[spots_here[at_place * 3 + j]]
             there = (s < count) & (keep[sources[s], c * 3 + j] == 1)
             out[block(s, j)] = jnp.where(there, found, jnp.zeros_like(found))
     for copy in started:
@@ -729,19 +761,21 @@
             pltpu.VMEM((rows, cols), F32),
             pltpu.VMEM((rows, cols), F32),
             pltpu.VMEM((rows, cols), F32),
-            pltpu.VMEM((8 * LIST, bs, bs), BF16),
+            pltpu.VMEM((16 * LIST, bs, bs), BF16),
             pltpu.VMEM((3, 8, bs), F32),
             pltpu.VMEM((2, 15, 8, bs), F32),
             pltpu.SMEM((16 * per * 3,), jnp.int32),
             pltpu.SMEM((8 * per * 3,), jnp.int32),
+            pltpu.SMEM((32,), jnp.int32),
+            pltpu.SMEM((32,), jnp.int32),
             dma((108,)),
-            dma((2, 2, 16)),
+            dma((2, 2, 2, 4)),
             dma((2, 4)),
             dma((2, 4)),
             dma((4,)),
             dma((4,)),
             dma((2, 15)),
-        ] + [pltpu.VMEM((LIST, bs, bs), BF16)] * 32,
+        ] + [pltpu.VMEM((4 * LIST, bs, bs), BF16)] * 4 + [pltpu.VMEM((BUNDLE, bs, bs), BF16)] * 16,
         compiler_params=pltpu.CompilerParams(
             collective_id=0, has_side_effects=True, vmem_limit_bytes=56 << 20
         ),
@@ -750,11 +784,15 @@
 
 def step(density, keep_mask, owner_map):
     rows = lax.axis_size("row")
-    cols = lax.axis_size("col")
     blocks = keep_mask.shape[0]
-    kept = keep_mask.reshape(rows, blocks // rows, cols, blocks // cols).sum(axis=(1, 3))
+    halves = keep_mask.reshape(rows, blocks // rows // 2, 2, 4, 4, 3).sum(axis=(1, 5))
+    upper, lower = halves[:, 0], halves[:, 1]
+    excess = jnp.maximum(
+        jnp.maximum(upper, lower) - LIST,
+        jnp.maximum(upper.sum(axis=2, keepdims=True), lower.sum(axis=1, keepdims=True)) - BUNDLE,
+    )
     return lax.cond(
-        jnp.max(kept) <= LIST, packed_step, dense_step, density, keep_mask, owner_map
+        jnp.max(excess) <= 0, packed_step, dense_step, density, keep_mask, owner_map
     ).astype(F32)
 
 

time: 114 us -> 111 us (0.974)
  Pallas kernels: 110 us -> 105 us
    pallas_call x1, Pallas kernels: 110 us -> 105 us  [packed_step(): pl.pallas_call(packed_kernel, out_shape=jax.ShapeDtypeStruct(((per + 2) *...]
where the time goes in v4:
time: 111 us
  Pallas kernels  105 us (95%)
  other arithmetic  3.29 us (3%)
  local copies, waits for them, and re-layouts  1.49 us (1%)
    pallas_call x1, Pallas kernels, packed_step(): pl.pallas_call(packed_kernel, out_shape=jax.ShapeDtypeStruct(((per + 2) *...  105 us

profile of v4, /device:TPU:1, one launch (start us, length us, event | category | flops | bytes accessed | tf_op | source)
XLA Modules:
  0.0 110.9 jit_solution(6688762291144128993)
XLA Ops:
  0.0 1.2 %reshape.8 = s32[8,3,2,4,4,3]{5,4,3,2,1,0:T(4,128)S(1)} reshape(s32[48,48]{1,0:T(8,128)} %param.6) | data formatting | bytes 18432 | tf_op jit(solution)/shard_map/reshape | solution.py:788
  1.2 1.2 %reduce_sum.27 = s32[8,2,4,4]{3,2,1,0:T(4,128)S(1)} reduce(s32[8,3,2,4,4,3]{5,4,3,2,1,0:T(4,128)S(1)} %reshape.8, s32[]{:T(128)} %constant.2.clone.1), dimensions={1,5}, to_apply=%region_0.0 | reduce | flops 2048 | bytes 10244 | tf_op jit(solution)/shard_map/reduce_sum | solution.py:788
  2.4 0.2 slice_reduce_fusion.1
  2.6 0.1 copy.6
  2.7 0.1 copy.7
  2.8 0.1 copy.5
  2.9 0.7 fusion
  4.2 105.5 %conditional.6 = (bf16[1024,384]{1,0:T(8,128)(2,1)S(1)}) conditional(s32[]{:T(128)} %convert_element_type.12, (f32[768,384]{1,0:T(8,128)}, s32[48,48]{1,0:T(8,128)}, s32[48]{0:T(128)}) %tuple.21, (f32[768,384]{1,0:T(8,128)}, s32[48,48]{1,0:T(8,128)}, s32[48]{0:T(128)}) %tuple.21), branch_computations={%region_4.0_spmd, %region_5.0_spmd} | conditional | bytes 8
  4.2 105.2 %branch_1_fun.1 = bf16[1024,384]{1,0:T(8,128)(2,1)S(1)} custom-call(f32[768,384]{1,0:T(8,128)} %get-tuple-element.29.dens, s32[48,48]{1,0:T(8,128)} %get-tuple-element.30.keep, s32[48]{0:T(128)} %get-tuple-element.31.owner), custom_call_target="tpu_custom_call" | custom-call | tf_op jit(solution)/shard_map/cond/branch_1_fun/pallas_call | solution.py:747
  109.7 1.2 %convert_element_type.13 = f32[1024,384]{1,0:T(8,128)} convert(bf16[1024,384]{1,0:T(8,128)(2,1)S(1)} %get-tuple-element.35) | non-fusion elementwise | flops 393216 | bytes 2359296 | tf_op jit(solution)/shard_map/convert_element_type | solution.py:796

commit v5 on v4

--- a/solution.py
+++ b/solution.py
@@ -540,26 +540,30 @@
     def columns(stage, col):
         return Ring(lambda source: col.at[pl.ds(2 * source, 2)], col_sem.at[stage], sib_sem.at[stage])
 
-    def column_of(place):
-        behind_y, behind_x = divmod(place, 4)
-        return lax.rem(y - sign * behind_y + 8, 4) * 4 + lax.rem(x - sign * behind_x + 8, 4)
-
-    def spread(bundles, h, place):
-        source = column_of(place)
-        start = offsets[h * 16 + source]
-        bundle = bundles[h][place // 4 if h == 0 else place % 4]
-        for i in range(h * per // 2, (h + 1) * per // 2):
-            for j in range(3):
-                spot = jnp.minimum(start + spots[source * tile + i * 3 + j], BUNDLE - 1)
-                found = bundle[spot]
-                there = keep[r * per + origin(i), source * 3 + j] == 1
-                left[block(i, j)] = jnp.where(there, found, jnp.zeros_like(found))
+    def spread(bundles, h, away):
+        behind = lax.rem((y if h == 0 else x) - sign * away + 8, 4)
+        bundle = bundles[h][away]
+        sources = [4 * behind + t if h == 0 else 4 * t + behind for t in range(4)]
+        for t, source in enumerate(sources):
+            start = offsets[h * 16 + source]
+            for i in range(per // 2):
+                for j in range(3):
+                    b = (h * per // 2 + i) * 3 + j
+                    spot = jnp.minimum(start + spots[source * tile + b], BUNDLE - 1)
+                    found = bundle[spot]
+                    there = keep[r * per + origin(b // 3), source * 3 + j] == 1
+                    left[block(i, 3 * t + j)] = jnp.where(there, found, jnp.zeros_like(found))
+        return sources
 
     fresh = set()
 
-    def add(name, total, h, place, col):
+    def add(name, total, h, sources, col):
         here = pl.ds(h * (rows // 2), rows // 2)
-        term = jnp.dot(left[here, :], col[column_of(place)], preferred_element_type=F32)
+        if h == 0:
+            right = col[pl.ds(sources[0], 4)].reshape(4 * cols, cols)
+        else:
+            right = jnp.concatenate([col[source] for source in sources], axis=0)
+        term = jnp.dot(left[...], right, preferred_element_type=F32)
         if (name, h) in fresh:
             total[here, :] += term
         else:
@@ -569,20 +573,18 @@
     waiting = []
     columns_ready = []
 
-    def first_product(h, place):
-        spread(bundle_c, h, place)
-        add("square", square, h, place, col_c)
-
-    def second_product(h, place):
-        spread(bundle_s, h, place)
-        add("cubic", cubic, h, place, col_c)
-        add("quartic", quartic, h, place, col_s)
+    def first_product(h, away):
+        sources = spread(bundle_c, h, away)
+        add("square", square, h, sources, col_c)
+
+    def second_product(h, away):
+        sources = spread(bundle_s, h, away)
+        add("cubic", cubic, h, sources, col_c)
+        add("quartic", quartic, h, sources, col_s)
 
     def ready_for(product):
         def ready(h, away):
-            for other in range(4):
-                place = 4 * away + other if h == 0 else 4 * other + away
-                waiting.append(lambda place=place: product(h, place))
+            waiting.append(lambda: product(h, away))
             if columns_ready:
                 pending.extend(waiting)
                 waiting.clear()
@@ -625,7 +627,7 @@
     rows_c.take(1, 1)
     ring_c.finish()
     now_columns()
-    work(12)
+    work(3)
     rows_c.take(1, 3)
     work(len(pending))
     rows_c.take(1, 2)
@@ -680,7 +682,7 @@
     reduce_start(1)
     ring_s.finish()
     now_columns()
-    work(8)
+    work(2)
     rows_s.take(1, 3)
     work(len(pending))
     rows_s.take(1, 2)
@@ -757,7 +759,7 @@
             pltpu.VMEM((per * 3, bs, bs), BF16),
             pltpu.VMEM((16, cols, cols), BF16),
             pltpu.VMEM((16, cols, cols), BF16),
-            pltpu.VMEM((rows, cols), BF16),
+            pltpu.VMEM((rows // 2, 4 * cols), BF16),
             pltpu.VMEM((rows, cols), F32),
             pltpu.VMEM((rows, cols), F32),
             pltpu.VMEM((rows, cols), F32),

time: 111 us -> 109 us (0.982)
  Pallas kernels: 105 us -> 103 us
    pallas_call x1, Pallas kernels: 105 us -> 103 us  [packed_step(): pl.pallas_call(packed_kernel, out_shape=jax.ShapeDtypeStruct(((per + 2) *...]
where the time goes in v5:
time: 109 us
  Pallas kernels  103 us (94%)
  other arithmetic  3.29 us (3%)
  local copies, waits for them, and re-layouts  1.49 us (1%)
    pallas_call x1, Pallas kernels, packed_step(): pl.pallas_call(packed_kernel, out_shape=jax.ShapeDtypeStruct(((per + 2) *...  103 us

profile of v5, /device:TPU:1, one launch (start us, length us, event | category | flops | bytes accessed | tf_op | source)
XLA Modules:
  0.0 108.8 jit_solution(11585244346567695622)
XLA Ops:
  0.0 1.2 %reshape.8 = s32[8,3,2,4,4,3]{5,4,3,2,1,0:T(4,128)S(1)} reshape(s32[48,48]{1,0:T(8,128)} %param.6) | data formatting | bytes 18432 | tf_op jit(solution)/shard_map/reshape | solution.py:790
  1.2 1.2 %reduce_sum.27 = s32[8,2,4,4]{3,2,1,0:T(4,128)S(1)} reduce(s32[8,3,2,4,4,3]{5,4,3,2,1,0:T(4,128)S(1)} %reshape.8, s32[]{:T(128)} %constant.2.clone.1), dimensions={1,5}, to_apply=%region_0.0 | reduce | flops 2048 | bytes 10244 | tf_op jit(solution)/shard_map/reduce_sum | solution.py:790
  2.4 0.2 slice_reduce_fusion.1
  2.6 0.1 copy.6
  2.7 0.1 copy.7
  2.8 0.1 copy.5
  2.9 0.7 fusion
  4.2 103.4 %conditional.6 = (bf16[1024,384]{1,0:T(8,128)(2,1)S(1)}) conditional(s32[]{:T(128)} %convert_element_type.12, (f32[768,384]{1,0:T(8,128)}, s32[48,48]{1,0:T(8,128)}, s32[48]{0:T(128)}) %tuple.21, (f32[768,384]{1,0:T(8,128)}, s32[48,48]{1,0:T(8,128)}, s32[48]{0:T(128)}) %tuple.21), branch_computations={%region_4.0_spmd, %region_5.0_spmd} | conditional | bytes 8
  4.2 103.1 %branch_1_fun.1 = bf16[1024,384]{1,0:T(8,128)(2,1)S(1)} custom-call(f32[768,384]{1,0:T(8,128)} %get-tuple-element.29.dens, s32[48,48]{1,0:T(8,128)} %get-tuple-element.30.keep, s32[48]{0:T(128)} %get-tuple-element.31.owner), custom_call_target="tpu_custom_call" | custom-call | tf_op jit(solution)/shard_map/cond/branch_1_fun/pallas_call | solution.py:749
  107.6 1.2 %convert_element_type.13 = f32[1024,384]{1,0:T(8,128)} convert(bf16[1024,384]{1,0:T(8,128)(2,1)S(1)} %get-tuple-element.35) | non-fusion elementwise | flops 393216 | bytes 2359296 | tf_op jit(solution)/shard_map/convert_element_type | solution.py:798

commit v6 on v5

--- a/solution.py
+++ b/solution.py
@@ -686,24 +686,30 @@
     rows_s.take(1, 3)
     work(len(pending))
     rows_s.take(1, 2)
-    work(len(pending))
     reduce_end(1)
-
     trace_cubic, trace_quartic, spread_sum = (
         jnp.sum(sums[2, n:n + 1], keepdims=True) for n in range(3)
     )
     electrons = F32(rows * 8 // 2)
     factor = (electrons - (4.0 * trace_cubic - 3.0 * trace_quartic)) / (spread_sum + 1e-06)
-    for i in range(per):
-        for j in range(3):
-            three, four = cubic[block(i, j)], quartic[block(i, j)]
-            value = 4.0 * three - 3.0 * four + factor * (square[block(i, j)] - 2.0 * three + four)
-            blocks[i * 3 + j] = (value * kept(i, j)).astype(BF16)
+
+    def move_ring(h):
+        return Ring(
+            lambda source: moved.at[pl.ds((2 * source + h) * LIST, LIST)],
+            end_sem.at[h], end_sib_sem.at[h],
+        )
+
+    rings_t = [move_ring(0), move_ring(1)]
     for h in range(2):
+        work(1)
+        for i in range(h * per // 2, (h + 1) * per // 2):
+            for j in range(3):
+                three, four = cubic[block(i, j)], quartic[block(i, j)]
+                value = 4.0 * three - 3.0 * four + factor * (square[block(i, j)] - 2.0 * three + four)
+                blocks[i * 3 + j] = (value * kept(i, j)).astype(BF16)
         for s in range(LIST):
             moved[(2 * r + h) * LIST + s] = blocks[listed[h][s]]
-    ring_t = Ring(lambda source: moved.at[pl.ds(2 * source * LIST, 2 * LIST)], end_sem, end_sib_sem)
-    ring_t.have(0)
+        rings_t[h].have(0)
 
     slots = out.shape[0] // bs
 
@@ -728,8 +734,11 @@
     count, sources = lax.fori_loop(
         0, 8 * per, place_rows, (jnp.int32(0), (jnp.int32(0),) * slots)
     )
-    ring_t.take(1, 3, 2)
-    ring_t.finish()
+    for away in (1, 3, 2):
+        for ring in rings_t:
+            ring.take(away)
+    for ring in rings_t:
+        ring.finish()
     for s in range(slots):
         for j in range(3):
             inner = sources[s] % per
@@ -774,8 +783,8 @@
             dma((2, 2, 2, 4)),
             dma((2, 4)),
             dma((2, 4)),
-            dma((4,)),
-            dma((4,)),
+            dma((2, 4)),
+            dma((2, 4)),
             dma((2, 15)),
         ] + [pltpu.VMEM((4 * LIST, bs, bs), BF16)] * 4 + [pltpu.VMEM((BUNDLE, bs, bs), BF16)] * 16,
         compiler_params=pltpu.CompilerParams(

time: 109 us -> 107 us (0.982)
  Pallas kernels: 103 us -> 101 us
    pallas_call x1, Pallas kernels: 103 us -> 101 us  [packed_step(): pl.pallas_call(packed_kernel, out_shape=jax.ShapeDtypeStruct(((per + 2) *...]
where the time goes in v6:
time: 107 us
  Pallas kernels  101 us (94%)
  other arithmetic  3.29 us (3%)
  local copies, waits for them, and re-layouts  1.49 us (1%)
    pallas_call x1, Pallas kernels, packed_step(): pl.pallas_call(packed_kernel, out_shape=jax.ShapeDtypeStruct(((per + 2) *...  101 us

profile of v6, /device:TPU:1, one launch (start us, length us, event | category | flops | bytes accessed | tf_op | source)
XLA Modules:
  0.0 107.0 jit_solution(16896114330804932500)
XLA Ops:
  0.0 1.2 %reshape.8 = s32[8,3,2,4,4,3]{5,4,3,2,1,0:T(4,128)S(1)} reshape(s32[48,48]{1,0:T(8,128)} %param.6) | data formatting | bytes 18432 | tf_op jit(solution)/shard_map/reshape | solution.py:799
  1.2 1.2 %reduce_sum.27 = s32[8,2,4,4]{3,2,1,0:T(4,128)S(1)} reduce(s32[8,3,2,4,4,3]{5,4,3,2,1,0:T(4,128)S(1)} %reshape.8, s32[]{:T(128)} %constant.2.clone.1), dimensions={1,5}, to_apply=%region_0.0 | reduce | flops 2048 | bytes 10244 | tf_op jit(solution)/shard_map/reduce_sum | solution.py:799
  2.4 0.2 slice_reduce_fusion.1
  2.6 0.1 copy.6
  2.7 0.1 copy.7
  2.8 0.1 copy.5
  2.9 0.7 fusion
  4.2 101.5 %conditional.6 = (bf16[1024,384]{1,0:T(8,128)(2,1)S(1)}) conditional(s32[]{:T(128)} %convert_element_type.12, (f32[768,384]{1,0:T(8,128)}, s32[48,48]{1,0:T(8,128)}, s32[48]{0:T(128)}) %tuple.21, (f32[768,384]{1,0:T(8,128)}, s32[48,48]{1,0:T(8,128)}, s32[48]{0:T(128)}) %tuple.21), branch_computations={%region_4.0_spmd, %region_5.0_spmd} | conditional | bytes 8
  4.2 101.3 %branch_1_fun.1 = bf16[1024,384]{1,0:T(8,128)(2,1)S(1)} custom-call(f32[768,384]{1,0:T(8,128)} %get-tuple-element.29.dens, s32[48,48]{1,0:T(8,128)} %get-tuple-element.30.keep, s32[48]{0:T(128)} %get-tuple-element.31.owner), custom_call_target="tpu_custom_call" | custom-call | tf_op jit(solution)/shard_map/cond/branch_1_fun/pallas_call | solution.py:758
  105.8 1.2 %convert_element_type.13 = f32[1024,384]{1,0:T(8,128)} convert(bf16[1024,384]{1,0:T(8,128)(2,1)S(1)} %get-tuple-element.35) | non-fusion elementwise | flops 393216 | bytes 2359296 | tf_op jit(solution)/shard_map/convert_element_type | solution.py:807
